TPU v7x, 32 devices: a whole 2x2x4 slice. The times are simulated.
32 devices in a mesh: girth: 4 (over y, x), wall: 8 (over z, core).
Axes of the slice: x: 2, y: 2, z: 4, core: 2. Of those that a mesh axis runs over, the one named last changes fastest.
Arguments:
- adjoint_start: float32 [6, 64, 128, 128], P(None, 'girth', 'wall'), may hold values from -6 to 6
- right_side: float32 [6, 64, 128, 128], P(None, 'girth', 'wall'), may hold values from -6 to 6
- pivot_inverse: bfloat16 [6, 6, 64, 128, 128], P(None, None, 'girth', 'wall'), may hold values from -1.5 to 1.5, as said below
- lower_coupling: bfloat16 [6, 6, 64, 128, 128], P(None, None, 'girth', 'wall'), may hold values from -1 to 1, as said below
- upper_coupling: bfloat16 [6, 6, 64, 128, 128], P(None, None, 'girth', 'wall'), may hold values from -1 to 1, as said below
- girth_coeff: bfloat16 [6, 64, 128, 128], P(None, 'girth', 'wall'), may hold values from 0.0059814453 to 0.023925781
- stream_coeff: bfloat16 [6, 64, 128, 128], P(None, 'girth', 'wall'), may hold values from 0.0029907227 to 0.011962891
Outputs:
- adjoint_out: float32 [6, 64, 128, 128], P(None, 'girth', 'wall')
Inputs may be any that keep to these rules, and one draw needn't show every extreme that they name: `pivot_inverse`: one 6 x 6 block for each cell. `lower_coupling`: one 6 x 6 block for each cell. `upper_coupling`: one 6 x 6 block for each cell.
All inputs are finite; a program needn't handle non-finite values.
Results may differ from a plain program's by a relative error of at most 0.0003.
Values sent between devices are 32-bit elements; how exact they have to be, the bound alone decides.
A program may use at most 128 MiB of HBM per device.

v0:
```python
import jax
import jax.numpy as jnp
from jax import lax
from jax.sharding import PartitionSpec as P

SWEEPS = 2


def from_behind(block, axis, distance):
    devices = range(lax.axis_size(axis))
    route = [(i - distance, i) for i in devices if i - distance in devices]
    return lax.ppermute(block, axis, route)


def with_halo(block, sides, width):
    for axis, dim in sides:
        count = lax.axis_size(axis)
        forward = [(i, i + 1) for i in range(count - 1)]
        forward.append((count - 1, 0))
        backward = [(target, source) for source, target in forward]
        low = lax.ppermute(
            lax.slice_in_dim(block, block.shape[dim] - width, None, axis=dim), axis, forward
        )
        high = lax.ppermute(lax.slice_in_dim(block, 0, width, axis=dim), axis, backward)
        block = jnp.concatenate([low, block, high], axis=dim)
    return block


def apply_blocks(blocks, vectors):
    return jnp.sum(blocks.astype(jnp.float32) * vectors[None], axis=1)


def wall_slice(values, wall_step):
    return lax.dynamic_index_in_dim(values, wall_step, values.ndim - 2, False)


def segment_map(couplings, source, upward):
    wall_cells = source.shape[2]
    start_vector = jnp.zeros_like(source[:, :, 0])
    identity_block = jnp.eye(couplings.shape[0], dtype=jnp.float32)[:, :, None, None]
    start_matrix = jnp.broadcast_to(
        identity_block,
        (couplings.shape[0], couplings.shape[1], couplings.shape[2], couplings.shape[4]),
    )

    def segment_advance(carried, wall_step):
        vector, matrix = carried
        blocks = wall_slice(couplings, wall_step).astype(jnp.float32)
        vector = wall_slice(source, wall_step) + apply_blocks(blocks, vector)
        matrix = jnp.sum(blocks[:, :, None] * matrix[None], axis=1)
        return ((vector, matrix), None)

    steps_order = jnp.arange(wall_cells, dtype=jnp.int32)
    (vector, matrix), unused = lax.scan(
        segment_advance, (start_vector, start_matrix), steps_order, reverse=not upward, unroll=8
    )
    return (matrix, vector)


def line_values(couplings, source, incoming, upward):

    def line_advance(vector, wall_step):
        vector = wall_slice(source, wall_step) + apply_blocks(
            wall_slice(couplings, wall_step), vector
        )
        return (vector, vector)

    steps_order = jnp.arange(source.shape[2], dtype=jnp.int32)
    unused, stacked = lax.scan(line_advance, incoming, steps_order, reverse=not upward, unroll=8)
    return jnp.moveaxis(stacked, 0, 2)


def incoming_tip(matrix, offset, upward):
    wall_size = lax.axis_size("wall")
    outgoing = offset
    incoming = jnp.zeros_like(offset)
    for relay_step in range(wall_size - 1):
        if upward:
            incoming = from_behind(outgoing, "wall", 1)
        else:
            incoming = from_behind(outgoing, "wall", -1)
        outgoing = apply_blocks(matrix, incoming) + offset
    return incoming


def neighbour_term(adjoint, girth_coeff, stream_coeff):
    girth_cells = adjoint.shape[1]
    widened = with_halo(adjoint, (("girth", 1),), 2)
    beside_pair = widened[:, 1 : girth_cells + 1] + widened[:, 3 : girth_cells + 3]
    distant_pair = widened[:, 0:girth_cells] + widened[:, 4 : girth_cells + 4]
    padded = jnp.pad(adjoint, ((0, 0), (0, 0), (0, 0), (1, 1)))
    streamwise = padded[..., :-2] + padded[..., 2:]
    return (
        girth_coeff.astype(jnp.float32) * (beside_pair - 0.25 * distant_pair)
        + stream_coeff.astype(jnp.float32) * streamwise
    )


def relax(
    adjoint, right_side, pivot_inverse, lower_coupling, upper_coupling, girth_coeff, stream_coeff
):
    neighbours = neighbour_term(adjoint, girth_coeff, stream_coeff)
    from_above = from_behind(adjoint[:, :, :1], "wall", -1)
    raised = jnp.concatenate([adjoint[:, :, 1:], from_above], axis=2)
    lifted = adjoint - apply_blocks(upper_coupling, raised)
    from_below = from_behind(lifted[:, :, -1:], "wall", 1)
    lowered = jnp.concatenate([from_below, lifted[:, :, :-1]], axis=2)
    source = apply_blocks(pivot_inverse, right_side + neighbours) - (
        lifted - apply_blocks(lower_coupling, lowered)
    )
    up_matrix, up_offset = segment_map(lower_coupling, source, True)
    entering_low = incoming_tip(up_matrix, up_offset, True)
    forward_values = line_values(lower_coupling, source, entering_low, True)
    down_matrix, down_offset = segment_map(upper_coupling, forward_values, False)
    entering_high = incoming_tip(down_matrix, down_offset, False)
    backward_values = line_values(upper_coupling, forward_values, entering_high, False)
    return adjoint + backward_values


def on_device(
    adjoint_start,
    right_side,
    pivot_inverse,
    lower_coupling,
    upper_coupling,
    girth_coeff,
    stream_coeff,
):
    adjoint = adjoint_start
    for repeat in range(SWEEPS):
        adjoint = relax(
            adjoint,
            right_side,
            pivot_inverse,
            lower_coupling,
            upper_coupling,
            girth_coeff,
            stream_coeff,
        )
    return adjoint


def solution(mesh):
    in_specs = (
        P(None, "girth", "wall", None),
        P(None, "girth", "wall", None),
        P(None, None, "girth", "wall", None),
        P(None, None, "girth", "wall", None),
        P(None, None, "girth", "wall", None),
        P(None, "girth", "wall", None),
        P(None, "girth", "wall", None),
    )
    out_specs = P(None, "girth", "wall", None)
    return jax.shard_map(
        on_device, mesh=mesh, in_specs=in_specs, out_specs=out_specs, check_vma=False
    )
```

profile of v0, /device:TPU:1, one launch (start us, length us, event | category | flops | bytes accessed | tf_op | source)
XLA Modules:
  0.0 646.2 jit_solution(14959094453118420701)
XLA Ops:
  23.2 52.2 %while.120 = (s32[]{:T(128)}, f32[6,16,128]{2,1,0:T(8,128)S(1)}, f32[6,6,16,128]{3,2,1,0:T(8,128)S(1)}, s32[2,8]{1,0:T(2,128)S(1)}, f32[6,16,16,128]{3,1,0,2:T(8...) while((s32[]{:T(128)}, f32[6,16,128]{2,1,0:T(8,128)S(1)}, ...), condition=%wide.region_20.21_spmd.clone, body=%wide.region_3.20_spmd.clone.sunk | while | flops 8859675 | bytes 13861467 | solution.py:54
  80.5 4.2 collective-permute-start.5
  86.0 4.2 collective-permute-start.6
  91.4 4.2 collective-permute-start.7
  96.9 4.2 collective-permute-start.8
  102.3 4.2 collective-permute-start.9
  107.8 4.4 collective-permute-start.10
  116.9 40.1 %while.116 = (s32[]{:T(128)}, f32[6,16,128]{2,1,0:T(8,128)S(1)}, f32[2,8,6,16,128]{4,3,2,1,0:T(8,128)}, s32[2,8]{1,0:T(2,128)S(1)}, f32[6,16,16,128]{3,1,0,2:T(8...) while((s32[]{:T(128)}, f32[6,16,128]{2,1,0:T(8,128)S(1)}, ...), condition=%wide.region_36.37_spmd, body=%wide.region_27.36_spmd.sunk | while | flops 1867801 | bytes 9831505 | solution.py:69
  157.1 65.5 %while.121 = (s32[]{:T(128)}, f32[6,16,128]{2,1,0:T(8,128)S(1)}, f32[6,6,16,128]{3,2,1,0:T(8,128)S(1)}, s32[2,8]{1,0:T(2,128)S(1)}, f32[6,16,16,128]{3,1,0,2:T(8...) while((s32[]{:T(128)}, f32[6,16,128]{2,1,0:T(8,128)S(1)}, ...), condition=%wide.region_54.55_spmd.clone, body=%wide.region_37.54_spmd.clone.sunk | while | flops 8859676 | bytes 13861479 | solution.py:54
  261.7 76.8 %while.117 = (s32[]{:T(128)}, f32[6,16,128]{2,1,0:T(8,128)S(1)}, f32[2,8,6,16,128]{4,1,0,3,2:T(8,128)}, s32[2,8]{1,0:T(2,128)S(1)}, f32[6,16,16,128]{3,1,0,2:T(8...) while((s32[]{:T(128)}, f32[6,16,128]{2,1,0:T(8,128)S(1)}, ...), condition=%wide.region_70.71_spmd, body=%wide.region_61.70_spmd.sunk | while | flops 1867802 | bytes 16122521 | solution.py:69
  277.6 8.2 %dynamic-slice_convert_fusion.37 = (f32[6,6,16,1,128]{4,3,2,1,0:T(1,128)S(1)}, f32[6,6,16,1,128]{4,3,2,1,0:T(1,128)S(1)}, f32[6,6,16,1,128]{4,3,2,1,0:T(1,128)S(...) fusion(bf16[6,6,16,16,128]{4,3,2,1,0:T(8,128)(2,1)} %get-tuple-, ...), kind=kLoop, calls=%fused_computation.51.clone.1 | loop fusion | flops 589824 | bytes 3538976 | tf_op jit(solution)/shard_map/while/body/eval_jaxpr/convert_element_type | solution.py:30
  316.2 7.8 %dynamic-slice_convert_fusion.37 = (f32[6,6,16,1,128]{4,3,2,1,0:T(1,128)S(1)}, f32[6,6,16,1,128]{4,3,2,1,0:T(1,128)S(1)}, f32[6,6,16,1,128]{4,3,2,1,0:T(1,128)S(...) fusion(bf16[6,6,16,16,128]{4,3,2,1,0:T(8,128)(2,1)} %get-tuple-, ...), kind=kLoop, calls=%fused_computation.51.clone.1 | loop fusion | flops 589824 | bytes 3538976 | tf_op jit(solution)/shard_map/while/body/eval_jaxpr/convert_element_type | solution.py:30
  348.2 6.1 collective-permute-start.21
  356.5 52.1 %while.122 = (s32[]{:T(128)}, f32[6,16,128]{2,1,0:T(8,128)S(1)}, f32[6,6,16,128]{3,2,1,0:T(8,128)S(1)}, s32[2,8]{1,0:T(2,128)S(1)}, f32[6,16,16,128]{3,1,0,2:T(8...) while((s32[]{:T(128)}, f32[6,16,128]{2,1,0:T(8,128)S(1)}, ...), condition=%wide.region_91.92_spmd.clone, body=%wide.region_74.91_spmd.clone.sunk | while | flops 8859675 | bytes 13861467 | solution.py:54
  408.6 4.2 collective-permute-start.22
  414.1 4.2 collective-permute-start.23
  419.5 4.2 collective-permute-start.24
  425.0 4.2 collective-permute-start.25
  430.4 4.2 collective-permute-start.26
  435.9 4.2 collective-permute-start.27
  441.4 4.2 collective-permute-start.28
  447.7 39.1 %while.118 = (s32[]{:T(128)}, f32[6,16,128]{2,1,0:T(8,128)S(1)}, f32[2,8,6,16,128]{4,3,2,1,0:T(8,128)}, s32[2,8]{1,0:T(2,128)S(1)}, f32[6,16,16,128]{3,1,0,2:T(8...) while((s32[]{:T(128)}, f32[6,16,128]{2,1,0:T(8,128)S(1)}, ...), condition=%wide.region_107.108_spmd, body=%wide.region_98.107_spmd.sunk | while | flops 1867801 | bytes 9831505 | solution.py:69
  487.0 52.1 %while.123 = (s32[]{:T(128)}, f32[6,16,128]{2,1,0:T(8,128)S(1)}, f32[6,6,16,128]{3,2,1,0:T(8,128)S(1)}, s32[2,8]{1,0:T(2,128)S(1)}, f32[6,16,16,128]{3,1,0,2:T(8...) while((s32[]{:T(128)}, f32[6,16,128]{2,1,0:T(8,128)S(1)}, ...), condition=%wide.region_125.126_spmd.clone, body=%wide.region_108.125_spmd.clone.sunk | while | flops 8859676 | bytes 23298692 | solution.py:54
  578.8 65.3 %while.119 = (s32[]{:T(128)}, f32[6,16,128]{2,1,0:T(8,128)S(1)}, f32[2,8,6,16,128]{4,1,0,3,2:T(8,128)}, s32[2,8]{1,0:T(2,128)S(1)}, f32[6,16,16,128]{3,1,0,2:T(8...) while((s32[]{:T(128)}, f32[6,16,128]{2,1,0:T(8,128)S(1)}, ...), condition=%wide.region_141.142_spmd, body=%wide.region_132.141_spmd.sunk | while | flops 1867802 | bytes 16122521 | solution.py:69
  (649 shorter events, 326.7 us)
Async XLA Ops:
  1.6 13.2 %collective-permute-start = (f32[6,2,16,128]{3,2,1,0:T(8,128)}, f32[6,2,16,128]{3,2,1,0:T(8,128)S(1)}, u32[]{:S(2)}, u32[]{:S(2)}) collective-permute-start(f32[6,2,16,128]{3,2,1,0:T(8,128)} %get-tuple-element.1043), channel_id=1, source_target_pairs={{0,8},{8,16},{16,24},{24,0},{1,9},{9,17},{17,25},{25,1},{2,10},{10... | collective-permute-start | bytes 294920 | tf_op jit(solution)/shard_map/ppermute | solution.py:21
  3.6 11.9 %collective-permute-start.1 = (f32[6,2,16,128]{3,2,1,0:T(8,128)S(1)}, f32[6,2,16,128]{3,2,1,0:T(8,128)S(1)}, u32[]{:S(2)}, u32[]{:S(2)}) collective-permute-start(f32[6,2,16,128]{3,2,1,0:T(8,128)S(1)} %get-tuple-element.1044), channel_id=1, source_target_pairs={{8,0},{16,8},{24,16},{0,24},{9,1},{17,9},{25,17},{1,25},{10,2},{18... | collective-permute-start | bytes 294920 | tf_op jit(solution)/shard_map/ppermute | solution.py:24
  6.2 7.9 %collective-permute-start.2 = (f32[6,16,1,128]{3,2,1,0:T(1,128)}, f32[6,16,1,128]{3,2,1,0:T(1,128)S(1)}, u32[]{:S(2)}, u32[]{:S(2)}) collective-permute-start(f32[6,16,1,128]{3,2,1,0:T(1,128)} %slice.537), channel_id=1, source_target_pairs={{1,0},{2,1},{3,2},{4,3},{5,4},{6,5},{7,6},{9,8},{10,9},{11,10},{12... | collective-permute-start | bytes 147464 | tf_op jit(solution)/shard_map/ppermute | solution.py:12
  80.5 5.4 collective-permute-start.5
  86.0 5.4 collective-permute-start.6
  91.4 5.4 collective-permute-start.7
  96.9 5.4 collective-permute-start.8
  102.3 5.4 collective-permute-start.9
  107.8 8.1 %collective-permute-start.10 = (f32[6,16,128]{2,1,0:T(8,128)S(1)}, f32[6,16,128]{2,1,0:T(8,128)S(1)}, u32[]{:S(2)}, u32[]{:S(2)}) collective-permute-start(f32[6,16,128]{2,1,0:T(8,128)S(1)} %add.1543), channel_id=1, source_target_pairs={{0,1},{1,2},{2,3},{3,4},{4,5},{5,6},{6,7},{8,9},{9,10},{10,11},{11... | collective-permute-start | bytes 147464 | tf_op jit(solution)/shard_map/ppermute | solution.py:12
  249.8 5.4 collective-permute-start.16
  255.3 5.4 collective-permute-start.17
  339.8 5.7 collective-permute-start.20
  348.2 7.0 %collective-permute-start.21 = (f32[6,16,1,128]{3,2,1,0:T(1,128)S(1)}, f32[6,16,1,128]{3,2,1,0:T(1,128)S(1)}, u32[]{:S(2)}, u32[]{:S(2)}) collective-permute-start(f32[6,16,1,128]{3,2,1,0:T(1,128)S(1)} %slice.598), channel_id=1, source_target_pairs={{0,1},{1,2},{2,3},{3,4},{4,5},{5,6},{6,7},{8,9},{9,10},{10,11},{11... | collective-permute-start | bytes 147464 | tf_op jit(solution)/shard_map/ppermute | solution.py:12
  408.6 5.4 collective-permute-start.22
  414.1 5.4 collective-permute-start.23
  419.5 5.4 collective-permute-start.24
  425.0 5.4 collective-permute-start.25
  430.4 5.4 collective-permute-start.26
  435.9 5.4 collective-permute-start.27
  441.4 5.4 collective-permute-start.28
  539.0 6.0 collective-permute-start.29
  545.1 5.5 collective-permute-start.30
  556.1 5.4 collective-permute-start.32
  561.6 5.4 collective-permute-start.33
  (38 other events, 328.0 us)
where the time goes:
time: 657 us; the launch traced here: 646 us
  loops' own time  241 us (37%)
  other arithmetic  190 us (29%)
  starting transfers between devices  107 us (16%)
  waiting for transfers between devices  67.6 us (10%)
  local copies, waits for them, and re-layouts  39.4 us (6%)
    another operation x4, loops' own time, line_values(): lax.scan(line_advance, incoming, steps_order, reverse=not upward, unroll=8)  121 us
    another operation x4, loops' own time, segment_map(): lax.scan(segment_advance, (start_vector, start_matrix), steps_order, reve...  120 us
    ppermute x32, starting transfers between devices, from_behind(): return lax.ppermute(block, axis, route)  101 us
    ppermute x32, waiting for transfers between devices, from_behind(): return lax.ppermute(block, axis, route)  66.1 us
    reduce_sum x158, other arithmetic, apply_blocks(): return jnp.sum(blocks.astype(jnp.float32) * vectors[None], axis=1)  51.1 us
    convert_element_type x8, other arithmetic, apply_blocks(): return jnp.sum(blocks.astype(jnp.float32) * vectors[None], axis=1)  32.6 us
    add x64, other arithmetic, line_advance(): wall_slice(source, wall_step)  26.7 us
    add x64, other arithmetic, segment_advance(): vector = wall_slice(source, wall_step) + apply_blocks(blocks, vector)  26.5 us
  transfers between devices with their start and end apart: 36, of which 32 were waited for; matrix products, arithmetic and copies ran while one was open for 2% of the time, Pallas kernels for 0%

commit v1 on v0

v1 whole, which is shorter than its diff:
```python
import functools

import jax
import jax.numpy as jnp
from jax import lax
from jax.experimental import pallas as pl
from jax.experimental.pallas import tpu as pltpu
from jax.sharding import PartitionSpec as P

SWEEPS = 2
HALO = 2
HALVES = 2
MESH = pl.DeviceIdType.MESH
F32 = jnp.float32


def block_product(column, vector):
    total = column(0) * vector[0][None]
    for j in range(1, vector.shape[0]):
        total = total + column(j) * vector[j][None]
    return total


def kernel(
    girth_size,
    wall_size,
    sizes,
    adj_hbm,
    rhs_hbm,
    piv_hbm,
    low_hbm,
    upp_hbm,
    gc_hbm,
    sc_hbm,
    out_ref,
    adj,
    rhs,
    piv,
    low,
    upp,
    gc,
    sc,
    couplings,
    work,
    own_map,
    pair_map,
    chip_map,
    own_tip,
    pair_tip,
    chip_tip,
    entering,
    start_tip,
    load_sem,
    halo_send,
    halo_recv,
    map_send,
    map_recv,
    tip_send,
    tip_recv,
    chain_send,
    chain_recv,
):
    nv, girth, wall, stream = sizes
    half = girth // HALVES
    chips = wall_size // 2
    my_girth = lax.axis_index("girth")
    my_wall = lax.axis_index("wall")
    chip = my_wall // 2
    core = lax.rem(my_wall, 2)
    right = (lax.rem(my_girth + 1, girth_size), my_wall)
    left = (lax.rem(my_girth + girth_size - 1, girth_size), my_wall)
    partner = (my_girth, chip * 2 + 1 - core)

    def on_chip(other_chip, other_core):
        return (my_girth, other_chip * 2 + other_core)

    body_rows = pl.ds(HALO * wall, girth * wall)
    loads = [
        pltpu.make_async_copy(adj_hbm, adj.at[0, :, body_rows, :], load_sem.at[0]),
        pltpu.make_async_copy(low_hbm, low, load_sem.at[1]),
        pltpu.make_async_copy(rhs_hbm, rhs, load_sem.at[2]),
        pltpu.make_async_copy(gc_hbm, gc, load_sem.at[3]),
        pltpu.make_async_copy(sc_hbm, sc, load_sem.at[4]),
        pltpu.make_async_copy(piv_hbm, piv, load_sem.at[5]),
        pltpu.make_async_copy(upp_hbm, upp, load_sem.at[6]),
    ]
    for load in loads:
        load.start()

    barrier = pltpu.get_barrier_semaphore()

    def greet(device):
        pl.semaphore_signal(barrier, inc=1, device_id=device, device_id_type=MESH)

    greet(left)
    greet(right)
    greet(partner)

    @pl.when(chip > 0)
    def _():
        greet(on_chip(chip - 1, core))

        @pl.when(core == 0)
        def _():
            greet(on_chip(chip - 1, 1))

    @pl.when(chip < chips - 1)
    def _():
        greet(on_chip(chip + 1, core))

        @pl.when(core == 1)
        def _():
            greet(on_chip(chip + 1, 0))

    from_below = jnp.where(chip > 0, 2 - core, 0)
    from_above = jnp.where(chip < chips - 1, 1 + core, 0)
    pl.semaphore_wait(barrier, 3 + from_below + from_above)

    def remote(src, dst, send_sem, recv_sem, device):
        return pltpu.make_async_remote_copy(
            src_ref=src,
            dst_ref=dst,
            send_sem=send_sem,
            recv_sem=recv_sem,
            device_id=device,
            device_id_type=MESH,
        )

    def halo_copies(sweep):
        field = adj.at[sweep]
        width = HALO * wall
        return [
            remote(
                field.at[:, pl.ds(width, width), :],
                field.at[:, pl.ds(width + girth * wall, width), :],
                halo_send.at[sweep, 0],
                halo_recv.at[sweep, 0],
                left,
            ),
            remote(
                field.at[:, pl.ds(girth * wall, width), :],
                field.at[:, pl.ds(0, width), :],
                halo_send.at[sweep, 1],
                halo_recv.at[sweep, 1],
                right,
            ),
        ]

    def layer(w):
        return pl.ds(pl.multiple_of(w * girth, girth), girth)

    def coupling_column(d, w):
        return lambda j: couplings[d, :, j, layer(w), :]

    def order(d, step):
        return step if d == 0 else wall - 1 - step

    def transpose_coupling(d, source):
        def one_girth(g, carry):
            couplings[d, :, :, pl.ds(g, wall, stride=girth), :] = source[:, :, g].astype(F32)
            return carry

        lax.fori_loop(0, girth, one_girth, 0)

    def map_copy(d):
        return remote(own_map.at[d], pair_map.at[d], map_send.at[d], map_recv.at[d], partner)

    def make_map(d):
        for k in range(0, nv, 2):

            def advance(step, columns):
                column = coupling_column(d, order(d, step))
                return tuple(block_product(column, c) for c in columns)

            first = coupling_column(d, order(d, 0))
            columns = lax.fori_loop(1, wall, advance, (first(k), first(k + 1)))
            own_map[d, :, k] = columns[0]
            own_map[d, :, k + 1] = columns[1]

        @pl.when(core == d)
        def _():
            map_copy(d).start()

    def make_chip_map(d):
        @pl.when(core != d)
        def _():
            map_copy(d).wait_recv()

            def one_column(k, carry):
                chip_map[d, :, k] = block_product(
                    lambda j: own_map[d, :, j], pair_map[d, :, k]
                )
                return carry

            lax.fori_loop(0, nv, one_column, 0)

    lane = lax.broadcasted_iota(jnp.int32, (nv, wall, stream), 2)

    def make_source(sweep, g):
        def girth_layer(offset):
            rows = pl.ds(pl.multiple_of((g + HALO + offset) * wall, wall), wall)
            return adj[sweep, :, rows, :]

        here = girth_layer(0)
        beside_pair = girth_layer(-1) + girth_layer(1)
        distant_pair = girth_layer(-2) + girth_layer(2)
        before = jnp.where(lane == 0, 0.0, pltpu.roll(here, 1, 2))
        after = jnp.where(lane == stream - 1, 0.0, pltpu.roll(here, stream - 1, 2))
        neighbours = gc[:, g].astype(F32) * (beside_pair - 0.25 * distant_pair) + sc[
            :, g
        ].astype(F32) * (before + after)
        loaded = rhs[:, g] + neighbours
        work[:, pl.ds(g, wall, stride=girth), :] = block_product(
            lambda j: piv[:, j, g].astype(F32), loaded
        )

    def make_sources(sweep):
        def body(g, carry):
            make_source(sweep, g)
            return carry

        lax.fori_loop(HALO, girth - HALO, body, 0)
        for copy in halo_copies(sweep):
            copy.wait_recv()
        lax.fori_loop(0, HALO, body, 0)
        lax.fori_loop(girth - HALO, girth, body, 0)

    def advance_line(d, step, vector):
        w = order(d, step)
        return w, work[:, layer(w), :] + block_product(coupling_column(d, w), vector)

    def find_tip(sweep, d):
        first = work[:, layer(order(d, 0)), :]
        tip = lax.fori_loop(1, wall, lambda step, v: advance_line(d, step, v)[1], first)
        for h in range(HALVES):
            own_tip[sweep, d, h] = tip[:, h * half : (h + 1) * half]

    def rows_of(h):
        return pl.ds(h * half, half)

    def tip_copy(sweep, d, h):
        return remote(
            own_tip.at[sweep, d, h],
            pair_tip.at[sweep, d, h],
            tip_send.at[sweep, d, h],
            tip_recv.at[sweep, d, h],
            partner,
        )

    def chain_copy(sweep, d, h, target_core):
        next_chip = chip + 1 if d == 0 else chip - 1
        return remote(
            chip_tip.at[sweep, d, h],
            entering.at[sweep, d, h],
            chain_send.at[sweep, d, h, target_core],
            chain_recv.at[sweep, d, h],
            on_chip(next_chip, target_core),
        )

    def has_previous(d):
        return chip > 0 if d == 0 else chip < chips - 1

    def has_next(d):
        return chip < chips - 1 if d == 0 else chip > 0

    def send_tips(sweep, d):
        @pl.when(core == d)
        def _():
            for h in range(HALVES):
                tip_copy(sweep, d, h).start()

    def run_chain(sweep, d):
        @pl.when(core != d)
        def _():
            for h in range(HALVES):
                tip_copy(sweep, d, h).wait_recv()
                chip_tip[sweep, d, h] = own_tip[sweep, d, h] + block_product(
                    lambda j: own_map[d, :, j, rows_of(h), :], pair_tip[sweep, d, h]
                )

        @pl.when(jnp.logical_not(has_previous(d)))
        def _():
            entering[sweep, d] = jnp.zeros_like(entering[sweep, d])

        for h in range(HALVES):

            @pl.when(has_previous(d))
            def _():
                chain_copy(sweep, d, h, d).wait_recv()

            @pl.when(jnp.logical_and(core != d, has_next(d)))
            def _():
                chip_tip[sweep, d, h] = chip_tip[sweep, d, h] + block_product(
                    lambda j: chip_map[d, :, j, rows_of(h), :], entering[sweep, d, h]
                )
                chain_copy(sweep, d, h, 1 - d).start()
                chain_copy(sweep, d, h, d).start()

        for h in range(HALVES):

            @pl.when(core == d)
            def _():
                start_tip[:, rows_of(h), :] = entering[sweep, d, h]

            @pl.when(core != d)
            def _():
                start_tip[:, rows_of(h), :] = pair_tip[sweep, d, h] + block_product(
                    lambda j: pair_map[d, :, j, rows_of(h), :], entering[sweep, d, h]
                )

    def solve_forward():
        def body(step, vector):
            w, vector = advance_line(0, step, vector)
            work[:, layer(w), :] = vector
            return vector

        lax.fori_loop(0, wall, body, start_tip[...])

    def solve_backward(store):
        def body(step, vector):
            w, vector = advance_line(1, step, vector)
            store(w, vector)
            return vector

        lax.fori_loop(0, wall, body, start_tip[...])

    loads[0].wait()
    for copy in halo_copies(0):
        copy.start()
    loads[1].wait()
    transpose_coupling(0, low)
    make_map(0)
    for load in loads[2:6]:
        load.wait()

    for sweep in range(SWEEPS):
        make_sources(sweep)
        find_tip(sweep, 0)
        send_tips(sweep, 0)
        if sweep == 0:
            make_chip_map(0)
            loads[6].wait()
            transpose_coupling(1, upp)
            make_map(1)
        run_chain(sweep, 0)
        solve_forward()
        find_tip(sweep, 1)
        send_tips(sweep, 1)
        if sweep == 0:
            make_chip_map(1)
        run_chain(sweep, 1)
        if sweep < SWEEPS - 1:

            def store(w, vector):
                adj[sweep + 1, :, pl.ds(HALO * wall + w, girth, stride=wall), :] = vector

            solve_backward(store)
            for copy in halo_copies(sweep + 1):
                copy.start()
        else:

            def store(w, vector):
                out_ref[:, pl.ds(w, girth, stride=wall), :] = vector

            solve_backward(store)

    for sweep in range(SWEEPS):
        for copy in halo_copies(sweep):
            copy.wait_send()
    for d in range(2):

        @pl.when(core == d)
        def _():
            map_copy(d).wait_send()
            for sweep in range(SWEEPS):
                for h in range(HALVES):
                    tip_copy(sweep, d, h).wait_send()

        @pl.when(jnp.logical_and(core != d, has_next(d)))
        def _():
            for sweep in range(SWEEPS):
                for h in range(HALVES):
                    chain_copy(sweep, d, h, 0).wait_send()
                    chain_copy(sweep, d, h, 1).wait_send()


def on_device(
    girth_size,
    wall_size,
    adjoint_start,
    right_side,
    pivot_inverse,
    lower_coupling,
    upper_coupling,
    girth_coeff,
    stream_coeff,
):
    nv, girth, wall, stream = adjoint_start.shape
    half = girth // HALVES
    flat = (nv, girth * wall, stream)
    blocks = (nv, nv, girth, wall, stream)
    tips = (SWEEPS, 2, HALVES, nv, half, stream)
    maps = (2, nv, nv, girth, stream)
    dma = pltpu.SemaphoreType.DMA
    out = pl.pallas_call(
        functools.partial(kernel, girth_size, wall_size, (nv, girth, wall, stream)),
        out_shape=jax.ShapeDtypeStruct(flat, F32),
        in_specs=[pl.BlockSpec(memory_space=pl.ANY)] * 7,
        out_specs=pl.BlockSpec(memory_space=pltpu.VMEM),
        scratch_shapes=[
            pltpu.VMEM((SWEEPS, nv, (girth + 2 * HALO) * wall, stream), F32),
            pltpu.VMEM((nv, girth, wall, stream), F32),
            pltpu.VMEM(blocks, jnp.bfloat16),
            pltpu.VMEM(blocks, jnp.bfloat16),
            pltpu.VMEM(blocks, jnp.bfloat16),
            pltpu.VMEM((nv, girth, wall, stream), jnp.bfloat16),
            pltpu.VMEM((nv, girth, wall, stream), jnp.bfloat16),
            pltpu.VMEM((2, nv, nv, wall * girth, stream), F32),
            pltpu.VMEM((nv, wall * girth, stream), F32),
            pltpu.VMEM(maps, F32),
            pltpu.VMEM(maps, F32),
            pltpu.VMEM(maps, F32),
            pltpu.VMEM(tips, F32),
            pltpu.VMEM(tips, F32),
            pltpu.VMEM(tips, F32),
            pltpu.VMEM(tips, F32),
            pltpu.VMEM((nv, girth, stream), F32),
            dma((7,)),
            dma((SWEEPS, 2)),
            dma((SWEEPS, 2)),
            dma((2,)),
            dma((2,)),
            dma((SWEEPS, 2, HALVES)),
            dma((SWEEPS, 2, HALVES)),
            dma((SWEEPS, 2, HALVES, 2)),
            dma((SWEEPS, 2, HALVES)),
        ],
        compiler_params=pltpu.CompilerParams(
            collective_id=0, has_side_effects=True, vmem_limit_bytes=48 * 2**20
        ),
    )(
        adjoint_start.reshape(flat),
        right_side,
        pivot_inverse,
        lower_coupling,
        upper_coupling,
        girth_coeff,
        stream_coeff,
    )
    return out.reshape(adjoint_start.shape)


def solution(mesh):
    in_specs = (
        P(None, "girth", "wall", None),
        P(None, "girth", "wall", None),
        P(None, None, "girth", "wall", None),
        P(None, None, "girth", "wall", None),
        P(None, None, "girth", "wall", None),
        P(None, "girth", "wall", None),
        P(None, "girth", "wall", None),
    )
    out_specs = P(None, "girth", "wall", None)
    return jax.shard_map(
        functools.partial(on_device, mesh.shape["girth"], mesh.shape["wall"]),
        mesh=mesh,
        in_specs=in_specs,
        out_specs=out_specs,
        check_vma=False,
    )
```

time: 657 us -> 68.6 us (0.10); the launches traced: 646 us -> 67.9 us
  loops' own time: 241 us -> 0 us
  other arithmetic: 190 us -> 0 us
  starting transfers between devices: 107 us -> 0 us
  waiting for transfers between devices: 67.6 us -> 0 us
  Pallas kernels: 0 us -> 61.1 us
  local copies, waits for them, and re-layouts: 39.4 us -> 6.8 us
    another operation x8 -> x0, loops' own time: 241 us -> none  [the longest x4 121 us: line_values(): lax.scan(line_advance, incoming, steps_order, reverse=not upward, unroll=8)]
    ppermute x36 -> x0, starting transfers between devices: 107 us -> none  [the longest x32 101 us: from_behind(): return lax.ppermute(block, axis, route)]
    ppermute x36 -> x0, waiting for transfers between devices: 67.6 us -> none  [the longest x32 66.1 us: from_behind(): return lax.ppermute(block, axis, route)]
    pallas_call x0 -> x1, Pallas kernels: none -> 61.1 us  [on_device(): pl.pallas_call(functools.partial(kernel, girth_size, wall_size, (nv, girt...]
    reduce_sum x222 -> x0, other arithmetic: 59.6 us -> none  [the longest x158 51.1 us: apply_blocks(): return jnp.sum(blocks.astype(jnp.float32) * vectors[None], axis=1)]
    add x154 -> x0, other arithmetic: 56.8 us -> none  [the longest x64 26.7 us: line_advance(): wall_slice(source, wall_step)]
    convert_element_type x17 -> x0, other arithmetic: 45.8 us -> none  [the longest x8 32.6 us: apply_blocks(): return jnp.sum(blocks.astype(jnp.float32) * vectors[None], axis=1)]
    while x64 -> x0, other arithmetic: 23.1 us -> none
  transfers between devices with their start and end apart: 36 -> 0, of which waited for: 32 -> 0; matrix products, arithmetic and copies ran while one was open for 2% -> 0% of each run, Pallas kernels for 0% -> 0%
where the time goes in v1:
time: 68.6 us; the launch traced here: 67.9 us
  Pallas kernels  61.1 us (89%)
  local copies, waits for them, and re-layouts  6.8 us (10%)
    pallas_call x1, Pallas kernels, on_device(): pl.pallas_call(functools.partial(kernel, girth_size, wall_size, (nv, girt...  61.1 us
    unnamed x11, local copies, waits for them, and re-layouts  6.8 us

profile of v1, /device:TPU:1, one launch (start us, length us, event | category | flops | bytes accessed | tf_op | source)
XLA Modules:
  0.0 67.9 jit_solution(3906876220332183727)
XLA Ops:
  0.0 0.0 copy-start
  0.0 1.7 %copy-done = bf16[6,6,16,16,128]{4,3,2,1,0:T(8,128)(2,1)S(1)} copy-done((bf16[6,6,16,16,128]{4,3,2,1,0:T(8,128)(2,1)S(1)}, bf16[6,6,16,16,128]{4,3,2,1,0:T(8,128)(2,1)}, u32[]{:S(2)}) %copy-start) | copy-done | bytes 2359320
  1.7 0.0 copy-start.1
  1.7 1.1 %copy-done.1 = f32[6,16,16,128]{3,2,1,0:T(8,128)S(1)} copy-done((f32[6,16,16,128]{3,2,1,0:T(8,128)S(1)}, f32[6,16,16,128]{3,2,1,0:T(8,128)}, u32[]{:S(2)}) %copy-start.1) | copy-done | bytes 786456
  2.8 0.0 copy-start.2
  2.8 1.1 %copy-done.2 = f32[6,16,16,128]{3,2,1,0:T(8,128)S(1)} copy-done((f32[6,16,16,128]{3,2,1,0:T(8,128)S(1)}, f32[6,16,16,128]{3,2,1,0:T(8,128)}, u32[]{:S(2)}) %copy-start.2) | copy-done | bytes 786456
  3.9 0.0 copy-start.3
  3.9 1.0 %copy-done.3 = bf16[6,16,16,128]{3,2,1,0:T(8,128)(2,1)S(1)} copy-done((bf16[6,16,16,128]{3,2,1,0:T(8,128)(2,1)S(1)}, bf16[6,16,16,128]{3,2,1,0:T(8,128)(2,1)}, u32[]{:S(2)}) %copy-start.3) | copy-done | bytes 393240
  4.9 0.0 copy-start.4
  4.9 1.0 %copy-done.4 = bf16[6,16,16,128]{3,2,1,0:T(8,128)(2,1)S(1)} copy-done((bf16[6,16,16,128]{3,2,1,0:T(8,128)(2,1)S(1)}, bf16[6,16,16,128]{3,2,1,0:T(8,128)(2,1)}, u32[]{:S(2)}) %copy-start.4) | copy-done | bytes 393240
  5.9 61.1 %shard_map.73 = f32[6,256,128]{2,1,0:T(8,128)S(1)} custom-call(f32[6,256,128]{2,1,0:T(8,128)S(1)} %bitcast.3, f32[6,16,16,128]{3,2,1,0:T(8,128)S(1)} %copy-done.2, bf16[6,6,16,16,128]{4,3,2,1,0:T(8,128)(2,1)S(1)} %copy-done, bf16[6,6,16,16,128]{4,3,2,1,0:T(8,128)(2,1)} %low_hbm.1, bf16[6,6,16,16,128]{4,3,2,1,0:T(8,128)(2,1)} %upp_hbm.1, ...), custom_call_target="tpu_custom_call" | custom-call | tf_op jit(solution)/shard_map/pallas_call | solution.py:405
  67.0 0.9 %copy.9 = f32[6,16,16,128]{3,2,1,0:T(8,128)} copy(f32[6,16,16,128]{3,2,1,0:T(8,128)S(1)} %bitcast.2) | data formatting | bytes 1572864
Async XLA Ops:
  0.0 1.7 %copy-start = (bf16[6,6,16,16,128]{4,3,2,1,0:T(8,128)(2,1)S(1)}, bf16[6,6,16,16,128]{4,3,2,1,0:T(8,128)(2,1)}, u32[]{:S(2)}) copy-start(bf16[6,6,16,16,128]{4,3,2,1,0:T(8,128)(2,1)} %piv_hbm.1) | copy-start | bytes 7077892
  1.7 1.1 %copy-start.1 = (f32[6,16,16,128]{3,2,1,0:T(8,128)S(1)}, f32[6,16,16,128]{3,2,1,0:T(8,128)}, u32[]{:S(2)}) copy-start(f32[6,16,16,128]{3,2,1,0:T(8,128)} %param.7) | copy-start | bytes 2359300
  2.8 1.1 %copy-start.2 = (f32[6,16,16,128]{3,2,1,0:T(8,128)S(1)}, f32[6,16,16,128]{3,2,1,0:T(8,128)}, u32[]{:S(2)}) copy-start(f32[6,16,16,128]{3,2,1,0:T(8,128)} %rhs_hbm.1) | copy-start | bytes 2359300
  3.9 1.0 %copy-start.3 = (bf16[6,16,16,128]{3,2,1,0:T(8,128)(2,1)S(1)}, bf16[6,16,16,128]{3,2,1,0:T(8,128)(2,1)}, u32[]{:S(2)}) copy-start(bf16[6,16,16,128]{3,2,1,0:T(8,128)(2,1)} %gc_hbm.1) | copy-start | bytes 1179652
  4.9 1.0 %copy-start.4 = (bf16[6,16,16,128]{3,2,1,0:T(8,128)(2,1)S(1)}, bf16[6,16,16,128]{3,2,1,0:T(8,128)(2,1)}, u32[]{:S(2)}) copy-start(bf16[6,16,16,128]{3,2,1,0:T(8,128)(2,1)} %sc_hbm.1) | copy-start | bytes 1179652

commit v2 on v1

--- a/solution.py
+++ b/solution.py
@@ -42,6 +42,7 @@
     sc,
     couplings,
     work,
+    staged,
     own_map,
     pair_map,
     chip_map,
@@ -114,7 +115,6 @@
 
     from_below = jnp.where(chip > 0, 2 - core, 0)
     from_above = jnp.where(chip < chips - 1, 1 + core, 0)
-    pl.semaphore_wait(barrier, 3 + from_below + from_above)
 
     def remote(src, dst, send_sem, recv_sem, device):
         return pltpu.make_async_remote_copy(
@@ -146,21 +146,19 @@
             ),
         ]
 
-    def layer(w):
-        return pl.ds(pl.multiple_of(w * girth, girth), girth)
-
     def coupling_column(d, w):
-        return lambda j: couplings[d, :, j, layer(w), :]
+        return lambda j: couplings[d, :, j, w]
 
     def order(d, step):
         return step if d == 0 else wall - 1 - step
 
     def transpose_coupling(d, source):
-        def one_girth(g, carry):
-            couplings[d, :, :, pl.ds(g, wall, stride=girth), :] = source[:, :, g].astype(F32)
+        def one_row(i, carry):
+            for j in range(nv):
+                couplings[d, i, j] = jnp.swapaxes(source[i, j].astype(F32), 0, 1)
             return carry
 
-        lax.fori_loop(0, girth, one_girth, 0)
+        lax.fori_loop(0, nv, one_row, 0)
 
     def map_copy(d):
         return remote(own_map.at[d], pair_map.at[d], map_send.at[d], map_recv.at[d], partner)
@@ -210,7 +208,7 @@
             :, g
         ].astype(F32) * (before + after)
         loaded = rhs[:, g] + neighbours
-        work[:, pl.ds(g, wall, stride=girth), :] = block_product(
+        staged[:, g] = block_product(
             lambda j: piv[:, j, g].astype(F32), loaded
         )
 
@@ -225,12 +223,18 @@
         lax.fori_loop(0, HALO, body, 0)
         lax.fori_loop(girth - HALO, girth, body, 0)
 
+        def one_variable(i, carry):
+            work[i] = jnp.swapaxes(staged[i], 0, 1)
+            return carry
+
+        lax.fori_loop(0, nv, one_variable, 0)
+
     def advance_line(d, step, vector):
         w = order(d, step)
-        return w, work[:, layer(w), :] + block_product(coupling_column(d, w), vector)
+        return w, work[:, w] + block_product(coupling_column(d, w), vector)
 
     def find_tip(sweep, d):
-        first = work[:, layer(order(d, 0)), :]
+        first = work[:, order(d, 0)]
         tip = lax.fori_loop(1, wall, lambda step, v: advance_line(d, step, v)[1], first)
         for h in range(HALVES):
             own_tip[sweep, d, h] = tip[:, h * half : (h + 1) * half]
@@ -308,27 +312,27 @@
                     lambda j: pair_map[d, :, j, rows_of(h), :], entering[sweep, d, h]
                 )
 
-    def solve_forward():
+    def solve(d):
         def body(step, vector):
-            w, vector = advance_line(0, step, vector)
-            work[:, layer(w), :] = vector
+            w, vector = advance_line(d, step, vector)
+            work[:, w] = vector
             return vector
 
         lax.fori_loop(0, wall, body, start_tip[...])
 
-    def solve_backward(store):
-        def body(step, vector):
-            w, vector = advance_line(1, step, vector)
-            store(w, vector)
-            return vector
-
-        lax.fori_loop(0, wall, body, start_tip[...])
-
+    def prepare_upper():
+        loads[6].wait()
+        transpose_coupling(1, upp)
+        make_map(1)
+
+    in_lower_half = chip < chips // 2
+
+    loads[1].wait()
+    transpose_coupling(0, low)
+    pl.semaphore_wait(barrier, 3 + from_below + from_above)
     loads[0].wait()
     for copy in halo_copies(0):
         copy.start()
-    loads[1].wait()
-    transpose_coupling(0, low)
     make_map(0)
     for load in loads[2:6]:
         load.wait()
@@ -339,30 +343,31 @@
         send_tips(sweep, 0)
         if sweep == 0:
             make_chip_map(0)
-            loads[6].wait()
-            transpose_coupling(1, upp)
-            make_map(1)
+            pl.when(jnp.logical_not(in_lower_half))(prepare_upper)
         run_chain(sweep, 0)
-        solve_forward()
+        solve(0)
+        if sweep == 0:
+            pl.when(in_lower_half)(prepare_upper)
         find_tip(sweep, 1)
         send_tips(sweep, 1)
         if sweep == 0:
             make_chip_map(1)
         run_chain(sweep, 1)
-        if sweep < SWEEPS - 1:
-
-            def store(w, vector):
-                adj[sweep + 1, :, pl.ds(HALO * wall + w, girth, stride=wall), :] = vector
-
-            solve_backward(store)
+        solve(1)
+        last = sweep == SWEEPS - 1
+
+        def one_variable(i, carry):
+            values = jnp.swapaxes(work[i], 0, 1)
+            if last:
+                out_ref[i] = values
+            else:
+                adj[sweep + 1, i, body_rows] = values.reshape(girth * wall, stream)
+            return carry
+
+        lax.fori_loop(0, nv, one_variable, 0)
+        if not last:
             for copy in halo_copies(sweep + 1):
                 copy.start()
-        else:
-
-            def store(w, vector):
-                out_ref[:, pl.ds(w, girth, stride=wall), :] = vector
-
-            solve_backward(store)
 
     for sweep in range(SWEEPS):
         for copy in halo_copies(sweep):
@@ -404,7 +409,7 @@
     dma = pltpu.SemaphoreType.DMA
     out = pl.pallas_call(
         functools.partial(kernel, girth_size, wall_size, (nv, girth, wall, stream)),
-        out_shape=jax.ShapeDtypeStruct(flat, F32),
+        out_shape=jax.ShapeDtypeStruct((nv, girth, wall, stream), F32),
         in_specs=[pl.BlockSpec(memory_space=pl.ANY)] * 7,
         out_specs=pl.BlockSpec(memory_space=pltpu.VMEM),
         scratch_shapes=[
@@ -415,8 +420,9 @@
             pltpu.VMEM(blocks, jnp.bfloat16),
             pltpu.VMEM((nv, girth, wall, stream), jnp.bfloat16),
             pltpu.VMEM((nv, girth, wall, stream), jnp.bfloat16),
-            pltpu.VMEM((2, nv, nv, wall * girth, stream), F32),
-            pltpu.VMEM((nv, wall * girth, stream), F32),
+            pltpu.VMEM((2, nv, nv, wall, girth, stream), F32),
+            pltpu.VMEM((nv, wall, girth, stream), F32),
+            pltpu.VMEM((nv, girth, wall, stream), F32),
             pltpu.VMEM(maps, F32),
             pltpu.VMEM(maps, F32),
             pltpu.VMEM(maps, F32),
@@ -436,7 +442,7 @@
             dma((SWEEPS, 2, HALVES)),
         ],
         compiler_params=pltpu.CompilerParams(
-            collective_id=0, has_side_effects=True, vmem_limit_bytes=48 * 2**20
+            collective_id=0, has_side_effects=True, vmem_limit_bytes=62 * 2**20
         ),
     )(
         adjoint_start.reshape(flat),
@@ -447,7 +453,7 @@
         girth_coeff,
         stream_coeff,
     )
-    return out.reshape(adjoint_start.shape)
+    return out
 
 
 def solution(mesh):

time: 68.6 us -> 61 us (0.89)
  local copies, waits for them, and re-layouts: 6.8 us -> 2.1 us
  Pallas kernels: 61.1 us -> 58.4 us
    unnamed x11 -> x1, local copies, waits for them, and re-layouts: 6.8 us -> 2.1 us
    pallas_call x1, Pallas kernels: 61.1 us -> 58.4 us  [on_device(): pl.pallas_call(functools.partial(kernel, girth_size, wall_size, (nv, girt...]
where the time goes in v2:
time: 61 us; the launch traced here: 60.5 us
  Pallas kernels  58.4 us (96%)
  local copies, waits for them, and re-layouts  2.1 us (3%)
    pallas_call x1, Pallas kernels, on_device(): pl.pallas_call(functools.partial(kernel, girth_size, wall_size, (nv, girt...  58.4 us
    unnamed x1, local copies, waits for them, and re-layouts  2.1 us

profile of v2, /device:TPU:1, one launch (start us, length us, event | category | flops | bytes accessed | tf_op | source)
XLA Modules:
  0.0 60.5 jit_solution(14036076996218893323)
XLA Ops:
  0.0 58.4 %shard_map.73 = f32[6,16,16,128]{3,2,1,0:T(8,128)} custom-call(f32[6,256,128]{2,1,0:T(8,128)} %bitcast.1, f32[6,16,16,128]{3,2,1,0:T(8,128)} %rhs_hbm.1, bf16[6,6,16,16,128]{4,3,2,1,0:T(8,128)(2,1)} %piv_hbm.1, bf16[6,6,16,16,128]{4,3,2,1,0:T(8,128)(2,1)} %low_hbm.1, bf16[6,6,16,16,128]{4,3,2,1,0:T(8,128)(2,1)} %upp_hbm.1, bf16[6,16,16,128]{3,2,1,0:T(8,128)(2,1)} %gc_hbm.1, ...), custom_call_target="tpu_custom_call" | custom-call | tf_op jit(solution)/shard_map/pallas_call | solution.py:410
  58.4 2.1 %copy.9 = f32[6,16,16,128]{3,2,1,0:T(8,128)} copy(f32[6,16,16,128]{3,2,1,0:T(8,128)} %shard_map.73) | data formatting | bytes 1572864

commit v3 on v2

--- a/solution.py
+++ b/solution.py
@@ -43,37 +43,57 @@
     couplings,
     work,
     staged,
-    own_map,
-    pair_map,
-    chip_map,
-    own_tip,
-    pair_tip,
-    chip_tip,
+    other_map,
+    half_map,
+    lead_map,
+    other_tip,
+    half_tip,
+    lead_tip,
+    pair_out,
     entering,
+    starts,
+    other_start,
     start_tip,
+    whole_column,
     load_sem,
     halo_send,
     halo_recv,
     map_send,
     map_recv,
+    lead_map_send,
+    lead_map_recv,
     tip_send,
     tip_recv,
-    chain_send,
-    chain_recv,
+    lead_send,
+    lead_recv,
+    pair_send,
+    pair_recv,
+    start_send,
+    start_recv,
 ):
     nv, girth, wall, stream = sizes
     half = girth // HALVES
-    chips = wall_size // 2
+    quads = wall_size // 4
     my_girth = lax.axis_index("girth")
     my_wall = lax.axis_index("wall")
     chip = my_wall // 2
     core = lax.rem(my_wall, 2)
+    quad = my_wall // 4
+    side = lax.rem(chip, 2)
     right = (lax.rem(my_girth + 1, girth_size), my_wall)
     left = (lax.rem(my_girth + girth_size - 1, girth_size), my_wall)
     partner = (my_girth, chip * 2 + 1 - core)
 
-    def on_chip(other_chip, other_core):
-        return (my_girth, other_chip * 2 + other_core)
+    def on_chip(other_chip):
+        return (my_girth, other_chip * 2 + core)
+
+    place = (core, 1 - core)
+    is_lead = (side == 0, side == 1)
+    is_first = (quad == 0, quad == quads - 1)
+    is_last = (quad == quads - 1, quad == 0)
+    mate = on_chip(quad * 2 + 1 - side)
+    my_rows = pl.ds(pl.multiple_of(core * half, half), half)
+    other_rows = pl.ds(pl.multiple_of((1 - core) * half, half), half)
 
     body_rows = pl.ds(HALO * wall, girth * wall)
     loads = [
@@ -96,25 +116,26 @@
     greet(left)
     greet(right)
     greet(partner)
-
-    @pl.when(chip > 0)
+    greet(mate)
+
+    @pl.when(quad > 0)
     def _():
-        greet(on_chip(chip - 1, core))
-
-        @pl.when(core == 0)
-        def _():
-            greet(on_chip(chip - 1, 1))
-
-    @pl.when(chip < chips - 1)
+        greet(on_chip(chip - 2))
+
+        @pl.when(side == 0)
+        def _():
+            greet(on_chip(chip - 1))
+
+    @pl.when(quad < quads - 1)
     def _():
-        greet(on_chip(chip + 1, core))
-
-        @pl.when(core == 1)
-        def _():
-            greet(on_chip(chip + 1, 0))
-
-    from_below = jnp.where(chip > 0, 2 - core, 0)
-    from_above = jnp.where(chip < chips - 1, 1 + core, 0)
+        greet(on_chip(chip + 2))
+
+        @pl.when(side == 1)
+        def _():
+            greet(on_chip(chip + 1))
+
+    from_below = jnp.where(quad > 0, 2 - side, 0)
+    from_above = jnp.where(quad < quads - 1, 1 + side, 0)
 
     def remote(src, dst, send_sem, recv_sem, device):
         return pltpu.make_async_remote_copy(
@@ -161,7 +182,9 @@
         lax.fori_loop(0, nv, one_row, 0)
 
     def map_copy(d):
-        return remote(own_map.at[d], pair_map.at[d], map_send.at[d], map_recv.at[d], partner)
+        return remote(
+            other_map.at[d], half_map.at[d, place[d]], map_send.at[d], map_recv.at[d], partner
+        )
 
     def make_map(d):
         for k in range(0, nv, 2):
@@ -172,25 +195,28 @@
 
             first = coupling_column(d, order(d, 0))
             columns = lax.fori_loop(1, wall, advance, (first(k), first(k + 1)))
-            own_map[d, :, k] = columns[0]
-            own_map[d, :, k + 1] = columns[1]
-
-        @pl.when(core == d)
-        def _():
-            map_copy(d).start()
-
-    def make_chip_map(d):
-        @pl.when(core != d)
-        def _():
-            map_copy(d).wait_recv()
-
+            for shift in range(2):
+                whole_column[...] = columns[shift]
+                half_map[d, place[d], :, k + shift] = whole_column[:, my_rows, :]
+                other_map[d, :, k + shift] = whole_column[:, other_rows, :]
+        map_copy(d).start()
+
+    def lead_map_copy(d):
+        return remote(
+            lead_map.at[d, 0], lead_map.at[d, 1], lead_map_send.at[d], lead_map_recv.at[d], mate
+        )
+
+    def make_lead_map(d):
+        @pl.when(jnp.logical_and(is_lead[d], jnp.logical_not(is_first[d])))
+        def _():
             def one_column(k, carry):
-                chip_map[d, :, k] = block_product(
-                    lambda j: own_map[d, :, j], pair_map[d, :, k]
+                lead_map[d, 0, :, k] = block_product(
+                    lambda j: half_map[d, 1, :, j], half_map[d, 0, :, k]
                 )
                 return carry
 
             lax.fori_loop(0, nv, one_column, 0)
+            lead_map_copy(d).start()
 
     lane = lax.broadcasted_iota(jnp.int32, (nv, wall, stream), 2)
 
@@ -236,81 +262,116 @@
     def find_tip(sweep, d):
         first = work[:, order(d, 0)]
         tip = lax.fori_loop(1, wall, lambda step, v: advance_line(d, step, v)[1], first)
-        for h in range(HALVES):
-            own_tip[sweep, d, h] = tip[:, h * half : (h + 1) * half]
-
-    def rows_of(h):
-        return pl.ds(h * half, half)
-
-    def tip_copy(sweep, d, h):
+        whole_column[...] = tip
+        half_tip[sweep, d, place[d]] = whole_column[:, my_rows, :]
+        other_tip[sweep, d] = whole_column[:, other_rows, :]
+        tip_copy(sweep, d).start()
+
+    def tip_copy(sweep, d):
         return remote(
-            own_tip.at[sweep, d, h],
-            pair_tip.at[sweep, d, h],
-            tip_send.at[sweep, d, h],
-            tip_recv.at[sweep, d, h],
+            other_tip.at[sweep, d],
+            half_tip.at[sweep, d, place[d]],
+            tip_send.at[sweep, d],
+            tip_recv.at[sweep, d],
             partner,
         )
 
-    def chain_copy(sweep, d, h, target_core):
-        next_chip = chip + 1 if d == 0 else chip - 1
+    def lead_copy(sweep, d):
         return remote(
-            chip_tip.at[sweep, d, h],
-            entering.at[sweep, d, h],
-            chain_send.at[sweep, d, h, target_core],
-            chain_recv.at[sweep, d, h],
-            on_chip(next_chip, target_core),
-        )
-
-    def has_previous(d):
-        return chip > 0 if d == 0 else chip < chips - 1
-
-    def has_next(d):
-        return chip < chips - 1 if d == 0 else chip > 0
-
-    def send_tips(sweep, d):
-        @pl.when(core == d)
-        def _():
-            for h in range(HALVES):
-                tip_copy(sweep, d, h).start()
-
-    def run_chain(sweep, d):
-        @pl.when(core != d)
-        def _():
-            for h in range(HALVES):
-                tip_copy(sweep, d, h).wait_recv()
-                chip_tip[sweep, d, h] = own_tip[sweep, d, h] + block_product(
-                    lambda j: own_map[d, :, j, rows_of(h), :], pair_tip[sweep, d, h]
-                )
-
-        @pl.when(jnp.logical_not(has_previous(d)))
-        def _():
-            entering[sweep, d] = jnp.zeros_like(entering[sweep, d])
-
-        for h in range(HALVES):
-
-            @pl.when(has_previous(d))
+            lead_tip.at[sweep, d, 0],
+            lead_tip.at[sweep, d, 1],
+            lead_send.at[sweep, d],
+            lead_recv.at[sweep, d],
+            mate,
+        )
+
+    def pair_copy(sweep, d, target):
+        sign = 1 if d == 0 else -1
+        return remote(
+            pair_out.at[sweep, d],
+            entering.at[sweep, d],
+            pair_send.at[sweep, d, target],
+            pair_recv.at[sweep, d],
+            on_chip(chip + sign * (target + 1)),
+        )
+
+    def start_copy(sweep, d):
+        return remote(
+            starts.at[sweep, d, 1 - place[d]],
+            other_start.at[sweep, d],
+            start_send.at[sweep, d],
+            start_recv.at[sweep, d],
+            partner,
+        )
+
+    def apply_half(d, which, vector):
+        return block_product(lambda j: half_map[d, which, :, j], vector)
+
+    def begin_chain(sweep, d):
+        if sweep == 0:
+            map_copy(d).wait_recv()
+        tip_copy(sweep, d).wait_recv()
+
+        @pl.when(is_lead[d])
+        def _():
+            lead_tip[sweep, d, 0] = half_tip[sweep, d, 1] + apply_half(
+                d, 1, half_tip[sweep, d, 0]
+            )
+            lead_copy(sweep, d).start()
+
+        if sweep == 0:
+            make_lead_map(d)
+
+    def finish_chain(sweep, d):
+        first = is_first[d]
+        later = jnp.logical_not(first)
+        trail = jnp.logical_not(is_lead[d])
+
+        @pl.when(trail)
+        def _():
+            lead_copy(sweep, d).wait_recv()
+
+        if sweep == 0:
+
+            @pl.when(jnp.logical_and(trail, later))
             def _():
-                chain_copy(sweep, d, h, d).wait_recv()
-
-            @pl.when(jnp.logical_and(core != d, has_next(d)))
-            def _():
-                chip_tip[sweep, d, h] = chip_tip[sweep, d, h] + block_product(
-                    lambda j: chip_map[d, :, j, rows_of(h), :], entering[sweep, d, h]
-                )
-                chain_copy(sweep, d, h, 1 - d).start()
-                chain_copy(sweep, d, h, d).start()
-
-        for h in range(HALVES):
-
-            @pl.when(core == d)
-            def _():
-                start_tip[:, rows_of(h), :] = entering[sweep, d, h]
-
-            @pl.when(core != d)
-            def _():
-                start_tip[:, rows_of(h), :] = pair_tip[sweep, d, h] + block_product(
-                    lambda j: pair_map[d, :, j, rows_of(h), :], entering[sweep, d, h]
-                )
+                lead_map_copy(d).wait_recv()
+
+        @pl.when(later)
+        def _():
+            pair_copy(sweep, d, 0).wait_recv()
+
+        @pl.when(jnp.logical_and(is_lead[d], first))
+        def _():
+            starts[sweep, d, 0] = jnp.zeros_like(starts[sweep, d, 0])
+
+        @pl.when(jnp.logical_and(is_lead[d], later))
+        def _():
+            starts[sweep, d, 0] = entering[sweep, d]
+
+        @pl.when(jnp.logical_and(trail, first))
+        def _():
+            starts[sweep, d, 0] = lead_tip[sweep, d, 1]
+
+        @pl.when(jnp.logical_and(trail, later))
+        def _():
+            starts[sweep, d, 0] = lead_tip[sweep, d, 1] + block_product(
+                lambda j: lead_map[d, 1, :, j], entering[sweep, d]
+            )
+
+        middle = half_tip[sweep, d, 0] + apply_half(d, 0, starts[sweep, d, 0])
+        starts[sweep, d, 1] = middle
+
+        @pl.when(jnp.logical_and(trail, jnp.logical_not(is_last[d])))
+        def _():
+            pair_out[sweep, d] = half_tip[sweep, d, 1] + apply_half(d, 1, middle)
+            pair_copy(sweep, d, 1).start()
+            pair_copy(sweep, d, 0).start()
+
+        start_copy(sweep, d).start()
+        start_tip[:, my_rows, :] = starts[sweep, d, place[d]]
+        start_copy(sweep, d).wait_recv()
+        start_tip[:, other_rows, :] = other_start[sweep, d]
 
     def solve(d):
         def body(step, vector):
@@ -325,11 +386,11 @@
         transpose_coupling(1, upp)
         make_map(1)
 
-    in_lower_half = chip < chips // 2
+    in_lower_half = quad < quads // 2
 
     loads[1].wait()
     transpose_coupling(0, low)
-    pl.semaphore_wait(barrier, 3 + from_below + from_above)
+    pl.semaphore_wait(barrier, 4 + from_below + from_above)
     loads[0].wait()
     for copy in halo_copies(0):
         copy.start()
@@ -340,19 +401,16 @@
     for sweep in range(SWEEPS):
         make_sources(sweep)
         find_tip(sweep, 0)
-        send_tips(sweep, 0)
+        begin_chain(sweep, 0)
         if sweep == 0:
-            make_chip_map(0)
             pl.when(jnp.logical_not(in_lower_half))(prepare_upper)
-        run_chain(sweep, 0)
+        finish_chain(sweep, 0)
         solve(0)
         if sweep == 0:
             pl.when(in_lower_half)(prepare_upper)
         find_tip(sweep, 1)
-        send_tips(sweep, 1)
-        if sweep == 0:
-            make_chip_map(1)
-        run_chain(sweep, 1)
+        begin_chain(sweep, 1)
+        finish_chain(sweep, 1)
         solve(1)
         last = sweep == SWEEPS - 1
 
@@ -373,20 +431,24 @@
         for copy in halo_copies(sweep):
             copy.wait_send()
     for d in range(2):
-
-        @pl.when(core == d)
-        def _():
-            map_copy(d).wait_send()
-            for sweep in range(SWEEPS):
-                for h in range(HALVES):
-                    tip_copy(sweep, d, h).wait_send()
-
-        @pl.when(jnp.logical_and(core != d, has_next(d)))
-        def _():
-            for sweep in range(SWEEPS):
-                for h in range(HALVES):
-                    chain_copy(sweep, d, h, 0).wait_send()
-                    chain_copy(sweep, d, h, 1).wait_send()
+        map_copy(d).wait_send()
+
+        @pl.when(jnp.logical_and(is_lead[d], jnp.logical_not(is_first[d])))
+        def _():
+            lead_map_copy(d).wait_send()
+
+        for sweep in range(SWEEPS):
+            tip_copy(sweep, d).wait_send()
+            start_copy(sweep, d).wait_send()
+
+            @pl.when(is_lead[d])
+            def _():
+                lead_copy(sweep, d).wait_send()
+
+            @pl.when(jnp.logical_and(jnp.logical_not(is_lead[d]), jnp.logical_not(is_last[d])))
+            def _():
+                pair_copy(sweep, d, 0).wait_send()
+                pair_copy(sweep, d, 1).wait_send()
 
 
 def on_device(
@@ -404,8 +466,8 @@
     half = girth // HALVES
     flat = (nv, girth * wall, stream)
     blocks = (nv, nv, girth, wall, stream)
-    tips = (SWEEPS, 2, HALVES, nv, half, stream)
-    maps = (2, nv, nv, girth, stream)
+    tip = (nv, half, stream)
+    half_blocks = (nv, nv, half, stream)
     dma = pltpu.SemaphoreType.DMA
     out = pl.pallas_call(
         functools.partial(kernel, girth_size, wall_size, (nv, girth, wall, stream)),
@@ -423,23 +485,33 @@
             pltpu.VMEM((2, nv, nv, wall, girth, stream), F32),
             pltpu.VMEM((nv, wall, girth, stream), F32),
             pltpu.VMEM((nv, girth, wall, stream), F32),
-            pltpu.VMEM(maps, F32),
-            pltpu.VMEM(maps, F32),
-            pltpu.VMEM(maps, F32),
-            pltpu.VMEM(tips, F32),
-            pltpu.VMEM(tips, F32),
-            pltpu.VMEM(tips, F32),
-            pltpu.VMEM(tips, F32),
+            pltpu.VMEM((2, *half_blocks), F32),
+            pltpu.VMEM((2, 2, *half_blocks), F32),
+            pltpu.VMEM((2, 2, *half_blocks), F32),
+            pltpu.VMEM((SWEEPS, 2, *tip), F32),
+            pltpu.VMEM((SWEEPS, 2, 2, *tip), F32),
+            pltpu.VMEM((SWEEPS, 2, 2, *tip), F32),
+            pltpu.VMEM((SWEEPS, 2, *tip), F32),
+            pltpu.VMEM((SWEEPS, 2, *tip), F32),
+            pltpu.VMEM((SWEEPS, 2, 2, *tip), F32),
+            pltpu.VMEM((SWEEPS, 2, *tip), F32),
+            pltpu.VMEM((nv, girth, stream), F32),
             pltpu.VMEM((nv, girth, stream), F32),
             dma((7,)),
             dma((SWEEPS, 2)),
             dma((SWEEPS, 2)),
             dma((2,)),
             dma((2,)),
-            dma((SWEEPS, 2, HALVES)),
-            dma((SWEEPS, 2, HALVES)),
-            dma((SWEEPS, 2, HALVES, 2)),
-            dma((SWEEPS, 2, HALVES)),
+            dma((2,)),
+            dma((2,)),
+            dma((SWEEPS, 2)),
+            dma((SWEEPS, 2)),
+            dma((SWEEPS, 2)),
+            dma((SWEEPS, 2)),
+            dma((SWEEPS, 2, 2)),
+            dma((SWEEPS, 2)),
+            dma((SWEEPS, 2)),
+            dma((SWEEPS, 2)),
         ],
         compiler_params=pltpu.CompilerParams(
             collective_id=0, has_side_effects=True, vmem_limit_bytes=62 * 2**20

time: 61 us -> 57.6 us (0.944)
  Pallas kernels: 58.4 us -> 55.3 us
    pallas_call x1, Pallas kernels: 58.4 us -> 55.3 us  [on_device(): pl.pallas_call(functools.partial(kernel, girth_size, wall_size, (nv, girt...]
where the time goes in v3:
time: 57.6 us; the launch traced here: 57.4 us
  Pallas kernels  55.3 us (96%)
  local copies, waits for them, and re-layouts  2.1 us (4%)
    pallas_call x1, Pallas kernels, on_device(): pl.pallas_call(functools.partial(kernel, girth_size, wall_size, (nv, girt...  55.3 us
    unnamed x1, local copies, waits for them, and re-layouts  2.1 us

profile of v3, /device:TPU:1, one launch (start us, length us, event | category | flops | bytes accessed | tf_op | source)
XLA Modules:
  0.0 57.4 jit_solution(10144436934239053220)
XLA Ops:
  0.0 55.3 %shard_map.73 = f32[6,16,16,128]{3,2,1,0:T(8,128)} custom-call(f32[6,256,128]{2,1,0:T(8,128)} %bitcast.1, f32[6,16,16,128]{3,2,1,0:T(8,128)} %rhs_hbm.1, bf16[6,6,16,16,128]{4,3,2,1,0:T(8,128)(2,1)} %piv_hbm.1, bf16[6,6,16,16,128]{4,3,2,1,0:T(8,128)(2,1)} %low_hbm.1, bf16[6,6,16,16,128]{4,3,2,1,0:T(8,128)(2,1)} %upp_hbm.1, bf16[6,16,16,128]{3,2,1,0:T(8,128)(2,1)} %gc_hbm.1, ...), custom_call_target="tpu_custom_call" | custom-call | tf_op jit(solution)/shard_map/pallas_call | solution.py:472
  55.4 2.1 %copy.9 = f32[6,16,16,128]{3,2,1,0:T(8,128)} copy(f32[6,16,16,128]{3,2,1,0:T(8,128)} %shard_map.73) | data formatting | bytes 1572864

commit v4 on v3

--- a/solution.py
+++ b/solution.py
@@ -46,6 +46,11 @@
     other_map,
     half_map,
     lead_map,
+    products,
+    other_cross,
+    half_cross,
+    chip_cross,
+    trial,
     other_tip,
     half_tip,
     lead_tip,
@@ -55,6 +60,8 @@
     other_start,
     start_tip,
     whole_column,
+    mate_start,
+    upper_answer,
     load_sem,
     halo_send,
     halo_recv,
@@ -62,6 +69,10 @@
     map_recv,
     lead_map_send,
     lead_map_recv,
+    cross_send,
+    cross_recv,
+    chip_cross_send,
+    chip_cross_recv,
     tip_send,
     tip_recv,
     lead_send,
@@ -186,20 +197,70 @@
             other_map.at[d], half_map.at[d, place[d]], map_send.at[d], map_recv.at[d], partner
         )
 
-    def make_map(d):
+    def keep_halves(column, half_ref, other_ref, k):
+        whole_column[...] = column
+        half_ref[:, k] = whole_column[:, my_rows, :]
+        other_ref[:, k] = whole_column[:, other_rows, :]
+
+    def make_lower_map():
+        first = coupling_column(0, 0)
         for k in range(0, nv, 2):
 
-            def advance(step, columns):
-                column = coupling_column(d, order(d, step))
-                return tuple(block_product(column, c) for c in columns)
-
-            first = coupling_column(d, order(d, 0))
+            def advance(w, columns):
+                column = coupling_column(0, w)
+                columns = tuple(block_product(column, c) for c in columns)
+                products[:, k, w] = columns[0]
+                products[:, k + 1, w] = columns[1]
+                return columns
+
+            products[:, k, 0] = first(k)
+            products[:, k + 1, 0] = first(k + 1)
             columns = lax.fori_loop(1, wall, advance, (first(k), first(k + 1)))
             for shift in range(2):
-                whole_column[...] = columns[shift]
-                half_map[d, place[d], :, k + shift] = whole_column[:, my_rows, :]
-                other_map[d, :, k + shift] = whole_column[:, other_rows, :]
-        map_copy(d).start()
+                keep_halves(
+                    columns[shift], half_map.at[0, place[0]], other_map.at[0], k + shift
+                )
+        map_copy(0).start()
+
+    def cross_copy():
+        return remote(
+            other_cross, half_cross.at[core], cross_send, cross_recv, partner
+        )
+
+    def chip_cross_copy():
+        return remote(
+            chip_cross.at[0], chip_cross.at[1], chip_cross_send, chip_cross_recv, mate
+        )
+
+    def make_upper_maps():
+        first = coupling_column(1, wall - 1)
+        for k in range(nv):
+
+            def advance(step, columns):
+                w = order(1, step)
+                column = coupling_column(1, w)
+                return (
+                    block_product(column, columns[0]),
+                    products[:, k, w] + block_product(column, columns[1]),
+                )
+
+            columns = lax.fori_loop(1, wall, advance, (first(k), products[:, k, wall - 1]))
+            keep_halves(columns[0], half_map.at[1, place[1]], other_map.at[1], k)
+            keep_halves(columns[1], half_cross.at[core], other_cross, k)
+        map_copy(1).start()
+        cross_copy().start()
+
+    def make_chip_cross():
+        @pl.when(is_lead[1])
+        def _():
+            def one_column(k, carry):
+                column = block_product(lambda j: half_cross[1, :, j], half_map[0, 0, :, k])
+                column = apply_half(1, 1, column)
+                chip_cross[0, :, k] = half_cross[0, :, k] + column
+                return carry
+
+            lax.fori_loop(0, nv, one_column, 0)
+            chip_cross_copy().start()
 
     def lead_map_copy(d):
         return remote(
@@ -259,13 +320,27 @@
         w = order(d, step)
         return w, work[:, w] + block_product(coupling_column(d, w), vector)
 
-    def find_tip(sweep, d):
-        first = work[:, order(d, 0)]
-        tip = lax.fori_loop(1, wall, lambda step, v: advance_line(d, step, v)[1], first)
+    def send_tip(sweep, d, tip):
         whole_column[...] = tip
         half_tip[sweep, d, place[d]] = whole_column[:, my_rows, :]
         other_tip[sweep, d] = whole_column[:, other_rows, :]
         tip_copy(sweep, d).start()
+
+    def find_lower_tip(sweep):
+        def body(w, vector):
+            vector = advance_line(0, w, vector)[1]
+            trial[:, w] = vector
+            return vector
+
+        trial[:, 0] = work[:, 0]
+        send_tip(sweep, 0, lax.fori_loop(1, wall, body, work[:, 0]))
+
+    def find_upper_tip(sweep):
+        def body(step, vector):
+            w = order(1, step)
+            return trial[:, w] + block_product(coupling_column(1, w), vector)
+
+        send_tip(sweep, 1, lax.fori_loop(1, wall, body, trial[:, wall - 1]))
 
     def tip_copy(sweep, d):
         return remote(
@@ -307,71 +382,151 @@
     def apply_half(d, which, vector):
         return block_product(lambda j: half_map[d, which, :, j], vector)
 
-    def begin_chain(sweep, d):
+    def apply_cross(which, vector):
+        return block_product(lambda j: half_cross[which, :, j], vector)
+
+    def begin_lower(sweep):
         if sweep == 0:
-            map_copy(d).wait_recv()
-        tip_copy(sweep, d).wait_recv()
-
-        @pl.when(is_lead[d])
-        def _():
-            lead_tip[sweep, d, 0] = half_tip[sweep, d, 1] + apply_half(
-                d, 1, half_tip[sweep, d, 0]
+            map_copy(0).wait_recv()
+        tip_copy(sweep, 0).wait_recv()
+
+        @pl.when(is_lead[0])
+        def _():
+            lead_tip[sweep, 0, 0] = half_tip[sweep, 0, 1] + apply_half(
+                0, 1, half_tip[sweep, 0, 0]
             )
-            lead_copy(sweep, d).start()
+            lead_copy(sweep, 0).start()
 
         if sweep == 0:
-            make_lead_map(d)
-
-    def finish_chain(sweep, d):
-        first = is_first[d]
-        later = jnp.logical_not(first)
-        trail = jnp.logical_not(is_lead[d])
+            make_lead_map(0)
+
+    def begin_upper(sweep):
+        if sweep == 0:
+            map_copy(1).wait_recv()
+            cross_copy().wait_recv()
+        tip_copy(sweep, 1).wait_recv()
+
+        @pl.when(is_lead[1])
+        def _():
+            reached = half_tip[sweep, 1, 0] + apply_cross(1, half_tip[sweep, 0, 0])
+            lead_tip[sweep, 1, 0] = half_tip[sweep, 1, 1] + apply_half(1, 1, reached)
+            lead_copy(sweep, 1).start()
+
+        if sweep == 0:
+            make_chip_cross()
+            make_lead_map(1)
+
+    def take_entering(sweep, d):
+        @pl.when(is_first[d])
+        def _():
+            entering[sweep, d] = jnp.zeros_like(entering[sweep, d])
+
+        @pl.when(jnp.logical_not(is_first[d]))
+        def _():
+            pair_copy(sweep, d, 0).wait_recv()
+
+    def apply_lead_map(d, which, vector):
+        return block_product(lambda j: lead_map[d, which, :, j], vector)
+
+    def finish_lower(sweep):
+        later = jnp.logical_not(is_first[0])
+        trail = jnp.logical_not(is_lead[0])
 
         @pl.when(trail)
         def _():
-            lead_copy(sweep, d).wait_recv()
+            lead_copy(sweep, 0).wait_recv()
 
         if sweep == 0:
 
             @pl.when(jnp.logical_and(trail, later))
             def _():
-                lead_map_copy(d).wait_recv()
-
-        @pl.when(later)
-        def _():
-            pair_copy(sweep, d, 0).wait_recv()
-
-        @pl.when(jnp.logical_and(is_lead[d], first))
-        def _():
-            starts[sweep, d, 0] = jnp.zeros_like(starts[sweep, d, 0])
-
-        @pl.when(jnp.logical_and(is_lead[d], later))
-        def _():
-            starts[sweep, d, 0] = entering[sweep, d]
-
-        @pl.when(jnp.logical_and(trail, first))
-        def _():
-            starts[sweep, d, 0] = lead_tip[sweep, d, 1]
+                lead_map_copy(0).wait_recv()
+
+        take_entering(sweep, 0)
+
+        @pl.when(is_lead[0])
+        def _():
+            starts[sweep, 0, 0] = entering[sweep, 0]
+
+        @pl.when(jnp.logical_and(trail, is_first[0]))
+        def _():
+            starts[sweep, 0, 0] = lead_tip[sweep, 0, 1]
 
         @pl.when(jnp.logical_and(trail, later))
         def _():
-            starts[sweep, d, 0] = lead_tip[sweep, d, 1] + block_product(
-                lambda j: lead_map[d, 1, :, j], entering[sweep, d]
+            starts[sweep, 0, 0] = lead_tip[sweep, 0, 1] + apply_lead_map(
+                0, 1, entering[sweep, 0]
             )
 
-        middle = half_tip[sweep, d, 0] + apply_half(d, 0, starts[sweep, d, 0])
-        starts[sweep, d, 1] = middle
-
-        @pl.when(jnp.logical_and(trail, jnp.logical_not(is_last[d])))
-        def _():
-            pair_out[sweep, d] = half_tip[sweep, d, 1] + apply_half(d, 1, middle)
-            pair_copy(sweep, d, 1).start()
-            pair_copy(sweep, d, 0).start()
-
-        start_copy(sweep, d).start()
+        middle = half_tip[sweep, 0, 0] + apply_half(0, 0, starts[sweep, 0, 0])
+        starts[sweep, 0, 1] = middle
+
+        @pl.when(jnp.logical_and(trail, jnp.logical_not(is_last[0])))
+        def _():
+            pair_out[sweep, 0] = half_tip[sweep, 0, 1] + apply_half(0, 1, middle)
+            pair_copy(sweep, 0, 1).start()
+            pair_copy(sweep, 0, 0).start()
+
+        start_copy(sweep, 0).start()
+
+    def finish_upper(sweep):
+        later = jnp.logical_not(is_first[1])
+        trail = jnp.logical_not(is_lead[1])
+
+        @pl.when(trail)
+        def _():
+            lead_copy(sweep, 1).wait_recv()
+            if sweep == 0:
+                chip_cross_copy().wait_recv()
+            mate_start[...] = lead_tip[sweep, 0, 0]
+
+        @pl.when(jnp.logical_and(trail, jnp.logical_not(is_first[0])))
+        def _():
+            mate_start[...] = mate_start[...] + apply_lead_map(0, 0, entering[sweep, 0])
+
+        @pl.when(trail)
+        def _():
+            starts[sweep, 1, 0] = lead_tip[sweep, 1, 1] + block_product(
+                lambda j: chip_cross[1, :, j], mate_start[...]
+            )
+
+        lower_answer = half_tip[sweep, 1, 0] + apply_cross(1, starts[sweep, 0, 1])
+        upper_answer[...] = half_tip[sweep, 1, 1] + apply_cross(0, starts[sweep, 0, 0])
+
+        if sweep == 0:
+
+            @pl.when(jnp.logical_and(trail, later))
+            def _():
+                lead_map_copy(1).wait_recv()
+
+        take_entering(sweep, 1)
+
+        @pl.when(is_lead[1])
+        def _():
+            starts[sweep, 1, 0] = entering[sweep, 1]
+
+        @pl.when(jnp.logical_and(trail, later))
+        def _():
+            starts[sweep, 1, 0] = starts[sweep, 1, 0] + apply_lead_map(
+                1, 1, entering[sweep, 1]
+            )
+
+        middle = lower_answer + apply_half(1, 0, starts[sweep, 1, 0])
+        starts[sweep, 1, 1] = middle
+
+        @pl.when(jnp.logical_and(trail, jnp.logical_not(is_last[1])))
+        def _():
+            pair_out[sweep, 1] = upper_answer[...] + apply_half(1, 1, middle)
+            pair_copy(sweep, 1, 1).start()
+            pair_copy(sweep, 1, 0).start()
+
+        start_copy(sweep, 1).start()
+
+    def solve_from_start(sweep, d):
         start_tip[:, my_rows, :] = starts[sweep, d, place[d]]
         start_copy(sweep, d).wait_recv()
         start_tip[:, other_rows, :] = other_start[sweep, d]
+        solve(d)
 
     def solve(d):
         def body(step, vector):
@@ -384,7 +539,9 @@
     def prepare_upper():
         loads[6].wait()
         transpose_coupling(1, upp)
-        make_map(1)
+        make_upper_maps()
+        find_upper_tip(0)
+        begin_upper(0)
 
     in_lower_half = quad < quads // 2
 
@@ -394,24 +551,35 @@
     loads[0].wait()
     for copy in halo_copies(0):
         copy.start()
-    make_map(0)
+    make_lower_map()
     for load in loads[2:6]:
         load.wait()
 
     for sweep in range(SWEEPS):
         make_sources(sweep)
-        find_tip(sweep, 0)
-        begin_chain(sweep, 0)
+        find_lower_tip(sweep)
+        if sweep > 0:
+            find_upper_tip(sweep)
+        begin_lower(sweep)
         if sweep == 0:
             pl.when(jnp.logical_not(in_lower_half))(prepare_upper)
-        finish_chain(sweep, 0)
-        solve(0)
+        else:
+            begin_upper(sweep)
+        finish_lower(sweep)
         if sweep == 0:
             pl.when(in_lower_half)(prepare_upper)
-        find_tip(sweep, 1)
-        begin_chain(sweep, 1)
-        finish_chain(sweep, 1)
-        solve(1)
+
+        @pl.when(jnp.logical_not(is_first[1]))
+        def _():
+            solve_from_start(sweep, 0)
+
+        finish_upper(sweep)
+
+        @pl.when(is_first[1])
+        def _():
+            solve_from_start(sweep, 0)
+
+        solve_from_start(sweep, 1)
         last = sweep == SWEEPS - 1
 
         def one_variable(i, carry):
@@ -430,6 +598,12 @@
     for sweep in range(SWEEPS):
         for copy in halo_copies(sweep):
             copy.wait_send()
+    cross_copy().wait_send()
+
+    @pl.when(is_lead[1])
+    def _():
+        chip_cross_copy().wait_send()
+
     for d in range(2):
         map_copy(d).wait_send()
 
@@ -488,6 +662,11 @@
             pltpu.VMEM((2, *half_blocks), F32),
             pltpu.VMEM((2, 2, *half_blocks), F32),
             pltpu.VMEM((2, 2, *half_blocks), F32),
+            pltpu.VMEM((nv, nv, wall, girth, stream), F32),
+            pltpu.VMEM(half_blocks, F32),
+            pltpu.VMEM((2, *half_blocks), F32),
+            pltpu.VMEM((2, *half_blocks), F32),
+            pltpu.VMEM((nv, wall, girth, stream), F32),
             pltpu.VMEM((SWEEPS, 2, *tip), F32),
             pltpu.VMEM((SWEEPS, 2, 2, *tip), F32),
             pltpu.VMEM((SWEEPS, 2, 2, *tip), F32),
@@ -497,6 +676,8 @@
             pltpu.VMEM((SWEEPS, 2, *tip), F32),
             pltpu.VMEM((nv, girth, stream), F32),
             pltpu.VMEM((nv, girth, stream), F32),
+            pltpu.VMEM(tip, F32),
+            pltpu.VMEM(tip, F32),
             dma((7,)),
             dma((SWEEPS, 2)),
             dma((SWEEPS, 2)),
@@ -504,6 +685,10 @@
             dma((2,)),
             dma((2,)),
             dma((2,)),
+            dma,
+            dma,
+            dma,
+            dma,
             dma((SWEEPS, 2)),
             dma((SWEEPS, 2)),
             dma((SWEEPS, 2)),

time: 57.6 us -> 55.1 us (0.957)
  Pallas kernels: 55.3 us -> 52.9 us
    pallas_call x1, Pallas kernels: 55.3 us -> 52.9 us  [on_device(): pl.pallas_call(functools.partial(kernel, girth_size, wall_size, (nv, girt...]
where the time goes in v4:
time: 55.1 us; the launch traced here: 55 us
  Pallas kernels  52.9 us (96%)
  local copies, waits for them, and re-layouts  2.1 us (4%)
    pallas_call x1, Pallas kernels, on_device(): pl.pallas_call(functools.partial(kernel, girth_size, wall_size, (nv, girt...  52.9 us
    unnamed x1, local copies, waits for them, and re-layouts  2.1 us

profile of v4, /device:TPU:1, one launch (start us, length us, event | category | flops | bytes accessed | tf_op | source)
XLA Modules:
  0.0 55.0 jit_solution(779171007542700048)
XLA Ops:
  0.0 52.9 %shard_map.73 = f32[6,16,16,128]{3,2,1,0:T(8,128)} custom-call(f32[6,256,128]{2,1,0:T(8,128)} %bitcast.1, f32[6,16,16,128]{3,2,1,0:T(8,128)} %rhs_hbm.1, bf16[6,6,16,16,128]{4,3,2,1,0:T(8,128)(2,1)} %piv_hbm.1, bf16[6,6,16,16,128]{4,3,2,1,0:T(8,128)(2,1)} %low_hbm.1, bf16[6,6,16,16,128]{4,3,2,1,0:T(8,128)(2,1)} %upp_hbm.1, bf16[6,16,16,128]{3,2,1,0:T(8,128)(2,1)} %gc_hbm.1, ...), custom_call_target="tpu_custom_call" | custom-call | tf_op jit(solution)/shard_map/pallas_call | solution.py:646
  52.9 2.1 %copy.9 = f32[6,16,16,128]{3,2,1,0:T(8,128)} copy(f32[6,16,16,128]{3,2,1,0:T(8,128)} %shard_map.73) | data formatting | bytes 1572864

commit v5 on v4

--- a/solution.py
+++ b/solution.py
@@ -15,10 +15,11 @@
 
 
 def block_product(column, vector):
-    total = column(0) * vector[0][None]
-    for j in range(1, vector.shape[0]):
-        total = total + column(j) * vector[j][None]
-    return total
+    terms = [column(j) * vector[j][None] for j in range(vector.shape[0])]
+    while len(terms) > 1:
+        pairs = [a + b for a, b in zip(terms[::2], terms[1::2])]
+        terms = pairs + terms[len(pairs) * 2 :]
+    return terms[0]
 
 
 def kernel(
@@ -181,6 +182,9 @@
     def coupling_column(d, w):
         return lambda j: couplings[d, :, j, w]
 
+    def line_loop(begin, body, carry):
+        return lax.fori_loop(begin, wall, body, carry, unroll=5 if begin else 4)
+
     def order(d, step):
         return step if d == 0 else wall - 1 - step
 
@@ -215,7 +219,7 @@
 
             products[:, k, 0] = first(k)
             products[:, k + 1, 0] = first(k + 1)
-            columns = lax.fori_loop(1, wall, advance, (first(k), first(k + 1)))
+            columns = line_loop(1, advance, (first(k), first(k + 1)))
             for shift in range(2):
                 keep_halves(
                     columns[shift], half_map.at[0, place[0]], other_map.at[0], k + shift
@@ -244,7 +248,7 @@
                     products[:, k, w] + block_product(column, columns[1]),
                 )
 
-            columns = lax.fori_loop(1, wall, advance, (first(k), products[:, k, wall - 1]))
+            columns = line_loop(1, advance, (first(k), products[:, k, wall - 1]))
             keep_halves(columns[0], half_map.at[1, place[1]], other_map.at[1], k)
             keep_halves(columns[1], half_cross.at[core], other_cross, k)
         map_copy(1).start()
@@ -333,14 +337,14 @@
             return vector
 
         trial[:, 0] = work[:, 0]
-        send_tip(sweep, 0, lax.fori_loop(1, wall, body, work[:, 0]))
+        send_tip(sweep, 0, line_loop(1, body, work[:, 0]))
 
     def find_upper_tip(sweep):
         def body(step, vector):
             w = order(1, step)
             return trial[:, w] + block_product(coupling_column(1, w), vector)
 
-        send_tip(sweep, 1, lax.fori_loop(1, wall, body, trial[:, wall - 1]))
+        send_tip(sweep, 1, line_loop(1, body, trial[:, wall - 1]))
 
     def tip_copy(sweep, d):
         return remote(
@@ -534,11 +538,9 @@
             work[:, w] = vector
             return vector
 
-        lax.fori_loop(0, wall, body, start_tip[...])
+        line_loop(0, body, start_tip[...])
 
     def prepare_upper():
-        loads[6].wait()
-        transpose_coupling(1, upp)
         make_upper_maps()
         find_upper_tip(0)
         begin_upper(0)
@@ -558,7 +560,10 @@
     for sweep in range(SWEEPS):
         make_sources(sweep)
         find_lower_tip(sweep)
-        if sweep > 0:
+        if sweep == 0:
+            loads[6].wait()
+            transpose_coupling(1, upp)
+        else:
             find_upper_tip(sweep)
         begin_lower(sweep)
         if sweep == 0:

time: 55.1 us -> 55.7 us (1.011)
  Pallas kernels: 52.9 us -> 53.5 us
    pallas_call x1, Pallas kernels: 52.9 us -> 53.5 us  [on_device(): pl.pallas_call(functools.partial(kernel, girth_size, wall_size, (nv, girt...]
where the time goes in v5:
time: 55.7 us; the launch traced here: 55.6 us
  Pallas kernels  53.5 us (96%)
  local copies, waits for them, and re-layouts  2.1 us (4%)
    pallas_call x1, Pallas kernels, on_device(): pl.pallas_call(functools.partial(kernel, girth_size, wall_size, (nv, girt...  53.5 us
    unnamed x1, local copies, waits for them, and re-layouts  2.1 us

profile of v5, /device:TPU:1, one launch (start us, length us, event | category | flops | bytes accessed | tf_op | source)
XLA Modules:
  0.0 55.6 jit_solution(1963872778419820138)
XLA Ops:
  0.0 53.5 %shard_map.73 = f32[6,16,16,128]{3,2,1,0:T(8,128)} custom-call(f32[6,256,128]{2,1,0:T(8,128)} %bitcast.1, f32[6,16,16,128]{3,2,1,0:T(8,128)} %rhs_hbm.1, bf16[6,6,16,16,128]{4,3,2,1,0:T(8,128)(2,1)} %piv_hbm.1, bf16[6,6,16,16,128]{4,3,2,1,0:T(8,128)(2,1)} %low_hbm.1, bf16[6,6,16,16,128]{4,3,2,1,0:T(8,128)(2,1)} %upp_hbm.1, bf16[6,16,16,128]{3,2,1,0:T(8,128)(2,1)} %gc_hbm.1, ...), custom_call_target="tpu_custom_call" | custom-call | tf_op jit(solution)/shard_map/pallas_call | solution.py:651
  53.5 2.1 %copy.9 = f32[6,16,16,128]{3,2,1,0:T(8,128)} copy(f32[6,16,16,128]{3,2,1,0:T(8,128)} %shard_map.73) | data formatting | bytes 1572864

commit v6 on v5

--- a/solution.py
+++ b/solution.py
@@ -183,16 +183,18 @@
         return lambda j: couplings[d, :, j, w]
 
     def line_loop(begin, body, carry):
-        return lax.fori_loop(begin, wall, body, carry, unroll=5 if begin else 4)
+        return lax.fori_loop(begin, wall, body, carry)
 
     def order(d, step):
         return step if d == 0 else wall - 1 - step
 
     def transpose_coupling(d, source):
         def one_row(i, carry):
-            for j in range(nv):
+            def one_block(j, inner):
                 couplings[d, i, j] = jnp.swapaxes(source[i, j].astype(F32), 0, 1)
-            return carry
+                return inner
+
+            return lax.fori_loop(0, nv, one_block, carry)
 
         lax.fori_loop(0, nv, one_row, 0)
 
@@ -208,7 +210,8 @@
 
     def make_lower_map():
         first = coupling_column(0, 0)
-        for k in range(0, nv, 2):
+        def two_columns(pair, carry):
+            k = 2 * pair
 
             def advance(w, columns):
                 column = coupling_column(0, w)
@@ -224,6 +227,9 @@
                 keep_halves(
                     columns[shift], half_map.at[0, place[0]], other_map.at[0], k + shift
                 )
+            return carry
+
+        lax.fori_loop(0, nv // 2, two_columns, 0)
         map_copy(0).start()
 
     def cross_copy():
@@ -238,7 +244,7 @@
 
     def make_upper_maps():
         first = coupling_column(1, wall - 1)
-        for k in range(nv):
+        def one_column(k, carry):
 
             def advance(step, columns):
                 w = order(1, step)
@@ -251,6 +257,9 @@
             columns = line_loop(1, advance, (first(k), products[:, k, wall - 1]))
             keep_halves(columns[0], half_map.at[1, place[1]], other_map.at[1], k)
             keep_halves(columns[1], half_cross.at[core], other_cross, k)
+            return carry
+
+        lax.fori_loop(0, nv, one_column, 0)
         map_copy(1).start()
         cross_copy().start()
 
@@ -567,12 +576,12 @@
             find_upper_tip(sweep)
         begin_lower(sweep)
         if sweep == 0:
-            pl.when(jnp.logical_not(in_lower_half))(prepare_upper)
+            pl.when(in_lower_half)(functools.partial(finish_lower, 0))
+            prepare_upper()
+            pl.when(jnp.logical_not(in_lower_half))(functools.partial(finish_lower, 0))
         else:
             begin_upper(sweep)
-        finish_lower(sweep)
-        if sweep == 0:
-            pl.when(in_lower_half)(prepare_upper)
+            finish_lower(sweep)
 
         @pl.when(jnp.logical_not(is_first[1]))
         def _():

time: 55.7 us -> 56.7 us (1.018)
  Pallas kernels: 53.5 us -> 54.5 us
    pallas_call x1, Pallas kernels: 53.5 us -> 54.5 us  [on_device(): pl.pallas_call(functools.partial(kernel, girth_size, wall_size, (nv, girt...]
where the time goes in v6:
time: 56.7 us; the launch traced here: 56.6 us
  Pallas kernels  54.5 us (96%)
  local copies, waits for them, and re-layouts  2.1 us (4%)
    pallas_call x1, Pallas kernels, on_device(): pl.pallas_call(functools.partial(kernel, girth_size, wall_size, (nv, girt...  54.5 us
    unnamed x1, local copies, waits for them, and re-layouts  2.1 us

profile of v6, /device:TPU:1, one launch (start us, length us, event | category | flops | bytes accessed | tf_op | source)
XLA Modules:
  0.0 56.6 jit_solution(8542475009111857708)
XLA Ops:
  0.0 54.5 %shard_map.73 = f32[6,16,16,128]{3,2,1,0:T(8,128)} custom-call(f32[6,256,128]{2,1,0:T(8,128)} %bitcast.1, f32[6,16,16,128]{3,2,1,0:T(8,128)} %rhs_hbm.1, bf16[6,6,16,16,128]{4,3,2,1,0:T(8,128)(2,1)} %piv_hbm.1, bf16[6,6,16,16,128]{4,3,2,1,0:T(8,128)(2,1)} %low_hbm.1, bf16[6,6,16,16,128]{4,3,2,1,0:T(8,128)(2,1)} %upp_hbm.1, bf16[6,16,16,128]{3,2,1,0:T(8,128)(2,1)} %gc_hbm.1, ...), custom_call_target="tpu_custom_call" | custom-call | tf_op jit(solution)/shard_map/pallas_call | solution.py:660
  54.5 2.1 %copy.9 = f32[6,16,16,128]{3,2,1,0:T(8,128)} copy(f32[6,16,16,128]{3,2,1,0:T(8,128)} %shard_map.73) | data formatting | bytes 1572864

commit v7 on v6

--- a/solution.py
+++ b/solution.py
@@ -15,11 +15,10 @@
 
 
 def block_product(column, vector):
-    terms = [column(j) * vector[j][None] for j in range(vector.shape[0])]
-    while len(terms) > 1:
-        pairs = [a + b for a, b in zip(terms[::2], terms[1::2])]
-        terms = pairs + terms[len(pairs) * 2 :]
-    return terms[0]
+    total = column(0) * vector[0][None]
+    for j in range(1, vector.shape[0]):
+        total = total + column(j) * vector[j][None]
+    return total
 
 
 def kernel(
@@ -183,18 +182,16 @@
         return lambda j: couplings[d, :, j, w]
 
     def line_loop(begin, body, carry):
-        return lax.fori_loop(begin, wall, body, carry)
+        return lax.fori_loop(begin, wall, body, carry, unroll=5 if begin else 4)
 
     def order(d, step):
         return step if d == 0 else wall - 1 - step
 
     def transpose_coupling(d, source):
         def one_row(i, carry):
-            def one_block(j, inner):
+            for j in range(nv):
                 couplings[d, i, j] = jnp.swapaxes(source[i, j].astype(F32), 0, 1)
-                return inner
-
-            return lax.fori_loop(0, nv, one_block, carry)
+            return carry
 
         lax.fori_loop(0, nv, one_row, 0)
 

time: 56.7 us -> 53.6 us (0.945)
  Pallas kernels: 54.5 us -> 51.4 us
    pallas_call x1, Pallas kernels: 54.5 us -> 51.4 us  [on_device(): pl.pallas_call(functools.partial(kernel, girth_size, wall_size, (nv, girt...]
where the time goes in v7:
time: 53.6 us; the launch traced here: 53.5 us
  Pallas kernels  51.4 us (96%)
  local copies, waits for them, and re-layouts  2.1 us (4%)
    pallas_call x1, Pallas kernels, on_device(): pl.pallas_call(functools.partial(kernel, girth_size, wall_size, (nv, girt...  51.4 us
    unnamed x1, local copies, waits for them, and re-layouts  2.1 us

profile of v7, /device:TPU:1, one launch (start us, length us, event | category | flops | bytes accessed | tf_op | source)
XLA Modules:
  0.0 53.5 jit_solution(11642856246980353186)
XLA Ops:
  0.0 51.4 %shard_map.73 = f32[6,16,16,128]{3,2,1,0:T(8,128)} custom-call(f32[6,256,128]{2,1,0:T(8,128)} %bitcast.1, f32[6,16,16,128]{3,2,1,0:T(8,128)} %rhs_hbm.1, bf16[6,6,16,16,128]{4,3,2,1,0:T(8,128)(2,1)} %piv_hbm.1, bf16[6,6,16,16,128]{4,3,2,1,0:T(8,128)(2,1)} %low_hbm.1, bf16[6,6,16,16,128]{4,3,2,1,0:T(8,128)(2,1)} %upp_hbm.1, bf16[6,16,16,128]{3,2,1,0:T(8,128)(2,1)} %gc_hbm.1, ...), custom_call_target="tpu_custom_call" | custom-call | tf_op jit(solution)/shard_map/pallas_call | solution.py:657
  51.4 2.1 %copy.9 = f32[6,16,16,128]{3,2,1,0:T(8,128)} copy(f32[6,16,16,128]{3,2,1,0:T(8,128)} %shard_map.73) | data formatting | bytes 1572864
